TPU v7x, 32 devices: a whole 2x2x4 slice. The times are simulated.
32 devices in a mesh: col: 8 (over z, x), sec: 4 (over y, core).
Axes of the slice: x: 2, y: 2, z: 4, core: 2. Of those that a mesh axis runs over, the one named last changes fastest.
Arguments:
- left_start: bfloat16 [2048, 6, 1024], P('sec'), may hold values from -6 to 6
- coupling: bfloat16 [8, 2048, 2304], P('col', 'sec'), may hold values from -0.125 to 0.125
- tensor: float32 [8, 6, 6, 6, 6], P('col'), may hold values from -1 to 1
- sketch: float32 [8, 6, 1024], P('col'), may hold values from -3 to 3
- block_parity: int32 [16], replicated, may hold values from 0 to 1
- leg_parity: int32 [8, 6], replicated, may hold values from 0 to 1, as said below
Outputs:
- states: bfloat16 [8, 2048, 6, 1024], P('col', 'sec')
- grams: float32 [8, 1024, 1024], P('col', 'sec')
Inputs may be any that keep to these rules, and one draw needn't show every extreme that they name: `leg_parity`: in each column exactly half of the 6 leg states are odd.
All inputs are finite; a program needn't handle non-finite values.
Results may differ from a plain program's by a relative error of at most 0.019.
Values may be sent and summed in bfloat16 or wider, within the bound.
No kernel may reach another device: no remote copies, remote signals or barrier semaphores. Data moves between devices by JAX's collectives and lax.ppermute only.
A program may use at most 192 MiB of HBM per device.

v0:
```python
import jax
import jax.numpy as jnp
from jax import lax
from jax.sharding import PartitionSpec as P

CHI = 2048
D = 6
PAN = 128


def padded_2(block, sides, width):
    for axis, dim in sides:
        count = lax.axis_size(axis)
        forward = [(i, i + 1) for i in range(count - 1)]
        backward = [(target, source) for source, target in forward]
        low = lax.ppermute(
            lax.slice_in_dim(block, block.shape[dim] - width, None, axis=dim), axis, forward
        )
        high = lax.ppermute(lax.slice_in_dim(block, 0, width, axis=dim), axis, backward)
        block = jnp.concatenate([low, block, high], axis=dim)
    return block


def shifted(block, axis, distance):
    devices = range(lax.axis_size(axis))
    route = [(i - distance, i) for i in devices if i - distance in devices]
    return lax.ppermute(block, axis, route)


def panel_signs(block_parity, leg_row, first_panel, panel_total):
    padded = jnp.pad(block_parity, (1, 1))
    window = lax.dynamic_slice_in_dim(padded, first_panel, panel_total, 0)
    odd_pairs = window.astype(jnp.float32)[:, None] * leg_row.astype(jnp.float32)[None, :]
    return 1.0 - 2.0 * odd_pairs


def advance(extended, mix_block, band_rows, sign_table):
    panel_total = sign_table.shape[0]
    panel_count = panel_total - 2
    leg_count = mix_block.shape[0]
    width = mix_block.shape[3]
    weighted = jnp.einsum(
        "adk,duek->auek", extended.astype(jnp.float32), mix_block, precision=lax.Precision.HIGHEST
    )
    weighted = weighted.reshape(panel_total, PAN, leg_count, leg_count * width)
    weighted = weighted * sign_table[:, None, :, None]
    weighted = weighted.astype(jnp.bfloat16).reshape(
        panel_total, PAN * leg_count, leg_count * width
    )
    summed = jnp.zeros((panel_count, PAN, leg_count * width), jnp.float32)
    for neighbour in range(3):
        summed = summed + jnp.einsum(
            "pbx,pxm->pbm",
            band_rows[:, :, neighbour],
            weighted[neighbour : neighbour + panel_count],
            preferred_element_type=jnp.float32,
        )
    return summed.astype(jnp.bfloat16).reshape(panel_count * PAN, leg_count, width)


def on_device(left_start, coupling, tensor, sketch, block_parity, leg_parity):
    row_count, leg_count, rank_total = left_start.shape
    panel_count = row_count // PAN
    col_count = lax.axis_size("col")
    sec_count = lax.axis_size("sec")
    col_index = lax.axis_index("col")
    first_panel = lax.axis_index("sec") * panel_count
    own_legs = lax.dynamic_index_in_dim(leg_parity, col_index, 0, keepdims=False)
    sign_table = panel_signs(block_parity, own_legs, first_panel, panel_count + 2)
    block_cols = 128
    block_count = rank_total // block_cols
    step_count = block_count + col_count - 1
    mixing = jnp.einsum("duez,zk->duek", tensor[0], sketch[0], precision=lax.Precision.HIGHEST)
    band_rows = coupling[0].reshape(panel_count, PAN, 3, PAN * leg_count)

    def turn(step_now, carry):
        received, sketch_out = carry
        block_now = step_now - col_index
        active = (block_now >= 0) & (block_now < block_count)
        offset = jnp.clip(block_now, 0, block_count - 1) * block_cols
        initial = lax.dynamic_slice_in_dim(left_start, offset, block_cols, 2)
        incoming = jnp.where(col_index == 0, initial, received)
        extended = padded_2(incoming, (("sec", 0),), PAN)
        mix_block = lax.dynamic_slice_in_dim(mixing, offset, block_cols, 3)
        produced = advance(extended, mix_block, band_rows, sign_table)
        updated = lax.dynamic_update_slice_in_dim(sketch_out, produced, offset, 2)
        sketch_out = jnp.where(active, updated, sketch_out)
        passed = shifted(produced, "col", 1)
        return (passed, sketch_out)

    start_carry = (
        jnp.zeros((row_count, leg_count, block_cols), jnp.bfloat16),
        jnp.zeros((row_count, leg_count, rank_total), jnp.bfloat16),
    )
    passed, sketch_out = lax.fori_loop(0, step_count, turn, start_carry)
    flattened = sketch_out.reshape(row_count * leg_count, rank_total)
    row_share = rank_total // sec_count
    partial_gram = jnp.einsum("xk,xm->km", flattened, flattened, preferred_element_type=jnp.float32)
    whole_gram = lax.psum(partial_gram.astype(jnp.bfloat16), "sec").astype(jnp.float32)
    own_rows = lax.dynamic_slice_in_dim(whole_gram, lax.axis_index("sec") * row_share, row_share, 0)
    gram_out = (own_rows / (CHI * D))[None]
    return (sketch_out[None], gram_out)


def solution(mesh):
    in_specs = (
        P("sec", None, None),
        P("col", "sec", None),
        P("col", None, None, None, None),
        P("col", None, None),
        P(),
        P(),
    )
    out_specs = (P("col", "sec", None, None), P("col", "sec", None))
    return jax.shard_map(
        on_device, mesh=mesh, in_specs=in_specs, out_specs=out_specs, check_vma=False
    )
```

profile of v0, /device:TPU:0, one launch (start us, length us, event | category | flops | bytes accessed | tf_op | source)
XLA Modules:
  0.0 1914.2 jit_solution(3755021114898824152)
XLA Ops:
  20.8 1818.2 %while.17 = (s32[]{:T(128)}, bf16[512,6,128]{0,2,1:T(8,128)(2,1)S(1)}, bf16[512,6,1024]{0,2,1:T(8,128)(2,1)}, s32[]{:T(128)}, f32[6,6,6,1024]{3,2,1,0:T(8,128)},...) while((s32[]{:T(128)}, ...), condition=%wide.region_1.2_spmd.clone, body=%wide.region_0.1_spmd.clone.sunk | while | flops 2079326336 | bytes 199914256 | solution.py:95
  45.5 18.8 copy.74
  64.3 18.0 reshape.47
  166.7 18.8 copy.74
  185.6 18.0 reshape.47
  287.4 18.8 copy.74
  306.3 18.0 reshape.47
  408.0 18.8 copy.74
  426.9 18.0 reshape.47
  529.5 18.8 copy.74
  548.4 18.0 reshape.47
  651.0 18.8 copy.74
  669.9 18.0 reshape.47
  772.5 18.8 copy.74
  791.3 18.0 reshape.47
  893.9 18.8 copy.74
  912.8 18.0 reshape.47
  1015.3 18.8 copy.74
  1034.1 18.0 reshape.47
  1136.5 18.8 copy.74
  1155.4 18.0 reshape.47
  1257.8 18.8 copy.74
  1276.6 18.0 reshape.47
  1379.0 18.8 copy.74
  1397.8 18.0 reshape.47
  1500.2 18.8 copy.74
  1519.0 18.0 reshape.47
  1621.4 18.8 copy.74
  1640.3 18.0 reshape.47
  1742.6 18.8 copy.74
  1761.5 18.0 reshape.47
  1859.3 46.0 %all-reduce.3.cloned.1.call-done = bf16[1024,1024]{1,0:T(8,128)(2,1)} async-done(((bf16[1024,1024]{1,0:T(8,128)(2,1)}), bf16[1024,1024]{1,0:T(8,128)(2,1)}) %all-reduce.3.cloned.1.call-update) | async-done | bytes 2097168 | tf_op jit(solution)/shard_map/psum | solution.py:99
  (453 shorter events, 1298.7 us)
Async XLA Ops:
  7.2 1898.1 %all-reduce.3.cloned.1.call-start = ((), (), s32[]{:S(2)}) async-start(), calls=%async_computation | async-start | bytes 4194304 | tf_op jit(solution)/shard_map/psum | solution.py:99
  24.6 7.9 collective-permute-start
  119.7 22.6 %collective-permute-start.2 = (bf16[512,6,128]{0,2,1:T(8,128)(2,1)S(1)}, bf16[512,6,128]{0,2,1:T(8,128)(2,1)S(1)}, u32[]{:S(2)}, u32[]{:S(2)}) collective-permute-start(bf16[512,6,128]{0,2,1:T(8,128)(2,1)S(1)} %reshape.48), channel_id=1, source_target_pairs={{0,4},{4,8},{8,12},{12,16},{16,20},{20,24},{24,28},{1,5},{5,9},{9,... | collective-permute-start | bytes 2359304 | tf_op jit(solution)/shard_map/while/body/eval_jaxpr/ppermute | solution.py:27
  145.8 7.9 collective-permute-start
  240.9 22.0 %collective-permute-start.2 = (bf16[512,6,128]{0,2,1:T(8,128)(2,1)S(1)}, bf16[512,6,128]{0,2,1:T(8,128)(2,1)S(1)}, u32[]{:S(2)}, u32[]{:S(2)}) collective-permute-start(bf16[512,6,128]{0,2,1:T(8,128)(2,1)S(1)} %reshape.48), channel_id=1, source_target_pairs={{0,4},{4,8},{8,12},{12,16},{16,20},{20,24},{24,28},{1,5},{5,9},{9,... | collective-permute-start | bytes 2359304 | tf_op jit(solution)/shard_map/while/body/eval_jaxpr/ppermute | solution.py:27
  266.5 7.9 collective-permute-start
  361.6 21.6 %collective-permute-start.2 = (bf16[512,6,128]{0,2,1:T(8,128)(2,1)S(1)}, bf16[512,6,128]{0,2,1:T(8,128)(2,1)S(1)}, u32[]{:S(2)}, u32[]{:S(2)}) collective-permute-start(bf16[512,6,128]{0,2,1:T(8,128)(2,1)S(1)} %reshape.48), channel_id=1, source_target_pairs={{0,4},{4,8},{8,12},{12,16},{16,20},{20,24},{24,28},{1,5},{5,9},{9,... | collective-permute-start | bytes 2359304 | tf_op jit(solution)/shard_map/while/body/eval_jaxpr/ppermute | solution.py:27
  386.8 8.2 collective-permute-start
  482.2 22.4 %collective-permute-start.2 = (bf16[512,6,128]{0,2,1:T(8,128)(2,1)S(1)}, bf16[512,6,128]{0,2,1:T(8,128)(2,1)S(1)}, u32[]{:S(2)}, u32[]{:S(2)}) collective-permute-start(bf16[512,6,128]{0,2,1:T(8,128)(2,1)S(1)} %reshape.48), channel_id=1, source_target_pairs={{0,4},{4,8},{8,12},{12,16},{16,20},{20,24},{24,28},{1,5},{5,9},{9,... | collective-permute-start | bytes 2359304 | tf_op jit(solution)/shard_map/while/body/eval_jaxpr/ppermute | solution.py:27
  508.2 8.3 collective-permute-start
  603.7 22.4 %collective-permute-start.2 = (bf16[512,6,128]{0,2,1:T(8,128)(2,1)S(1)}, bf16[512,6,128]{0,2,1:T(8,128)(2,1)S(1)}, u32[]{:S(2)}, u32[]{:S(2)}) collective-permute-start(bf16[512,6,128]{0,2,1:T(8,128)(2,1)S(1)} %reshape.48), channel_id=1, source_target_pairs={{0,4},{4,8},{8,12},{12,16},{16,20},{20,24},{24,28},{1,5},{5,9},{9,... | collective-permute-start | bytes 2359304 | tf_op jit(solution)/shard_map/while/body/eval_jaxpr/ppermute | solution.py:27
  629.7 8.3 collective-permute-start
  725.2 22.4 %collective-permute-start.2 = (bf16[512,6,128]{0,2,1:T(8,128)(2,1)S(1)}, bf16[512,6,128]{0,2,1:T(8,128)(2,1)S(1)}, u32[]{:S(2)}, u32[]{:S(2)}) collective-permute-start(bf16[512,6,128]{0,2,1:T(8,128)(2,1)S(1)} %reshape.48), channel_id=1, source_target_pairs={{0,4},{4,8},{8,12},{12,16},{16,20},{20,24},{24,28},{1,5},{5,9},{9,... | collective-permute-start | bytes 2359304 | tf_op jit(solution)/shard_map/while/body/eval_jaxpr/ppermute | solution.py:27
  751.2 8.3 collective-permute-start
  846.7 22.3 %collective-permute-start.2 = (bf16[512,6,128]{0,2,1:T(8,128)(2,1)S(1)}, bf16[512,6,128]{0,2,1:T(8,128)(2,1)S(1)}, u32[]{:S(2)}, u32[]{:S(2)}) collective-permute-start(bf16[512,6,128]{0,2,1:T(8,128)(2,1)S(1)} %reshape.48), channel_id=1, source_target_pairs={{0,4},{4,8},{8,12},{12,16},{16,20},{20,24},{24,28},{1,5},{5,9},{9,... | collective-permute-start | bytes 2359304 | tf_op jit(solution)/shard_map/while/body/eval_jaxpr/ppermute | solution.py:27
  872.6 8.3 collective-permute-start
  968.1 22.3 %collective-permute-start.2 = (bf16[512,6,128]{0,2,1:T(8,128)(2,1)S(1)}, bf16[512,6,128]{0,2,1:T(8,128)(2,1)S(1)}, u32[]{:S(2)}, u32[]{:S(2)}) collective-permute-start(bf16[512,6,128]{0,2,1:T(8,128)(2,1)S(1)} %reshape.48), channel_id=1, source_target_pairs={{0,4},{4,8},{8,12},{12,16},{16,20},{20,24},{24,28},{1,5},{5,9},{9,... | collective-permute-start | bytes 2359304 | tf_op jit(solution)/shard_map/while/body/eval_jaxpr/ppermute | solution.py:27
  994.0 8.3 collective-permute-start
  995.2 7.0 collective-permute-start.1
  1089.5 22.2 %collective-permute-start.2 = (bf16[512,6,128]{0,2,1:T(8,128)(2,1)S(1)}, bf16[512,6,128]{0,2,1:T(8,128)(2,1)S(1)}, u32[]{:S(2)}, u32[]{:S(2)}) collective-permute-start(bf16[512,6,128]{0,2,1:T(8,128)(2,1)S(1)} %reshape.48), channel_id=1, source_target_pairs={{0,4},{4,8},{8,12},{12,16},{16,20},{20,24},{24,28},{1,5},{5,9},{9,... | collective-permute-start | bytes 2359304 | tf_op jit(solution)/shard_map/while/body/eval_jaxpr/ppermute | solution.py:27
  1115.2 8.3 collective-permute-start
  1210.7 22.1 %collective-permute-start.2 = (bf16[512,6,128]{0,2,1:T(8,128)(2,1)S(1)}, bf16[512,6,128]{0,2,1:T(8,128)(2,1)S(1)}, u32[]{:S(2)}, u32[]{:S(2)}) collective-permute-start(bf16[512,6,128]{0,2,1:T(8,128)(2,1)S(1)} %reshape.48), channel_id=1, source_target_pairs={{0,4},{4,8},{8,12},{12,16},{16,20},{20,24},{24,28},{1,5},{5,9},{9,... | collective-permute-start | bytes 2359304 | tf_op jit(solution)/shard_map/while/body/eval_jaxpr/ppermute | solution.py:27
  1236.5 8.3 collective-permute-start
  1332.0 22.2 %collective-permute-start.2 = (bf16[512,6,128]{0,2,1:T(8,128)(2,1)S(1)}, bf16[512,6,128]{0,2,1:T(8,128)(2,1)S(1)}, u32[]{:S(2)}, u32[]{:S(2)}) collective-permute-start(bf16[512,6,128]{0,2,1:T(8,128)(2,1)S(1)} %reshape.48), channel_id=1, source_target_pairs={{0,4},{4,8},{8,12},{12,16},{16,20},{20,24},{24,28},{1,5},{5,9},{9,... | collective-permute-start | bytes 2359304 | tf_op jit(solution)/shard_map/while/body/eval_jaxpr/ppermute | solution.py:27
  1357.7 8.3 collective-permute-start
  1453.2 22.2 %collective-permute-start.2 = (bf16[512,6,128]{0,2,1:T(8,128)(2,1)S(1)}, bf16[512,6,128]{0,2,1:T(8,128)(2,1)S(1)}, u32[]{:S(2)}, u32[]{:S(2)}) collective-permute-start(bf16[512,6,128]{0,2,1:T(8,128)(2,1)S(1)} %reshape.48), channel_id=1, source_target_pairs={{0,4},{4,8},{8,12},{12,16},{16,20},{20,24},{24,28},{1,5},{5,9},{9,... | collective-permute-start | bytes 2359304 | tf_op jit(solution)/shard_map/while/body/eval_jaxpr/ppermute | solution.py:27
  1478.9 8.3 collective-permute-start
  1574.4 22.2 %collective-permute-start.2 = (bf16[512,6,128]{0,2,1:T(8,128)(2,1)S(1)}, bf16[512,6,128]{0,2,1:T(8,128)(2,1)S(1)}, u32[]{:S(2)}, u32[]{:S(2)}) collective-permute-start(bf16[512,6,128]{0,2,1:T(8,128)(2,1)S(1)} %reshape.48), channel_id=1, source_target_pairs={{0,4},{4,8},{8,12},{12,16},{16,20},{20,24},{24,28},{1,5},{5,9},{9,... | collective-permute-start | bytes 2359304 | tf_op jit(solution)/shard_map/while/body/eval_jaxpr/ppermute | solution.py:27
  1600.1 8.3 collective-permute-start
  1695.6 22.1 %collective-permute-start.2 = (bf16[512,6,128]{0,2,1:T(8,128)(2,1)S(1)}, bf16[512,6,128]{0,2,1:T(8,128)(2,1)S(1)}, u32[]{:S(2)}, u32[]{:S(2)}) collective-permute-start(bf16[512,6,128]{0,2,1:T(8,128)(2,1)S(1)} %reshape.48), channel_id=1, source_target_pairs={{0,4},{4,8},{8,12},{12,16},{16,20},{20,24},{24,28},{1,5},{5,9},{9,... | collective-permute-start | bytes 2359304 | tf_op jit(solution)/shard_map/while/body/eval_jaxpr/ppermute | solution.py:27
  1721.3 8.3 collective-permute-start
  1816.8 22.2 %collective-permute-start.2 = (bf16[512,6,128]{0,2,1:T(8,128)(2,1)S(1)}, bf16[512,6,128]{0,2,1:T(8,128)(2,1)S(1)}, u32[]{:S(2)}, u32[]{:S(2)}) collective-permute-start(bf16[512,6,128]{0,2,1:T(8,128)(2,1)S(1)} %reshape.48), channel_id=1, source_target_pairs={{0,4},{4,8},{8,12},{12,16},{16,20},{20,24},{24,28},{1,5},{5,9},{9,... | collective-permute-start | bytes 2359304 | tf_op jit(solution)/shard_map/while/body/eval_jaxpr/ppermute | solution.py:27
  (47 other events, 269.9 us)
Sparse Core Ops, SparseCore 0:
  1850.8 54.4 all-reduce.2
where the time goes:
time: 1930 us; the launch traced here: 1910 us
  local copies, waits for them, and re-layouts  916 us (47%)
  matrix products  357 us (18%)
  waiting for transfers between devices  270 us (14%)
  other arithmetic  200 us (10%)
  starting transfers between devices  155 us (8%)
    transpose x15, local copies, waits for them, and re-layouts, advance(): jnp.einsum('adk,duek->auek', extended.astype(jnp.float32), mix_block, pre...  283 us
    reshape x15, local copies, waits for them, and re-layouts, advance(): weighted = weighted.reshape(panel_total, PAN, leg_count, leg_count * width)  271 us
    slice x60, local copies, waits for them, and re-layouts, advance(): weighted[neighbour:neighbour + panel_count]  253 us
    ppermute x15, waiting for transfers between devices, shifted(): return lax.ppermute(block, axis, route)  224 us
    dot_general x15, matrix products, advance(): jnp.einsum('adk,duek->auek', extended.astype(jnp.float32), mix_block, pre...  196 us
    dot_general x45, matrix products, advance(): jnp.einsum('pbx,pxm->pbm', band_rows[:, :, neighbour], weighted[neighbour...  147 us
    convert_element_type x15, other arithmetic, advance(): weighted.astype(jnp.bfloat16)  144 us
    ppermute x15, starting transfers between devices, shifted(): return lax.ppermute(block, axis, route)  75.4 us
  transfers between devices with their start and end apart: 46, of which 16 were waited for; matrix products, arithmetic and copies ran while one was open for 4% of the time, Pallas kernels for 0%

commit v1 on v0

v1 whole, which is shorter than its diff:
```python
import functools

import jax
import jax.numpy as jnp
from jax import lax
from jax.experimental import pallas as pl
from jax.experimental.pallas import tpu as pltpu
from jax.sharding import PartitionSpec as P

CHI = 2048
D = 6
PAN = 128
KB = 64
PAIRS = D // 2
LANES = PAIRS * 2 * KB
STACK = D * PAN
BAND = 3 * PAN
TERMS = D * PAIRS * D
MIB = 1024 * 1024


def ordering_matrix():
    row = lax.broadcasted_iota(jnp.int32, (STACK, STACK), 0)
    col = lax.broadcasted_iota(jnp.int32, (STACK, STACK), 1)
    return (col == (row % D) * PAN + row // D).astype(jnp.bfloat16)


def order_kernel(sign_ref, band_ref, perm_ref, out_ref):
    p, w = pl.program_id(0), pl.program_id(1)
    moved = jnp.dot(band_ref[...], perm_ref[...], preferred_element_type=jnp.float32)
    for u in range(D):
        part = moved[:, u * PAN : (u + 1) * PAN] * sign_ref[p, w * D + u]
        out_ref[0, u * PAN : (u + 1) * PAN, :] = part.astype(jnp.bfloat16)


def ordered_coupling(coupling, signs):
    rows = coupling.shape[0]
    panels = rows // PAN
    return pl.pallas_call(
        order_kernel,
        grid=(panels, 3),
        in_specs=[
            pl.BlockSpec(memory_space=pltpu.SMEM),
            pl.BlockSpec((PAN, STACK), lambda p, w: (p, w)),
            pl.BlockSpec((STACK, STACK), lambda p, w: (0, 0)),
        ],
        out_specs=pl.BlockSpec((1, STACK, PAN), lambda p, w: (p, 0, w)),
        out_shape=jax.ShapeDtypeStruct((panels, STACK, BAND), jnp.bfloat16),
        compiler_params=pltpu.CompilerParams(vmem_limit_bytes=32 * MIB),
        name="order_coupling",
    )(signs, coupling, ordering_matrix())


def mix_rows(y_ref, mix_ref, column, res_ref):
    lane = lax.broadcasted_iota(jnp.int32, (4, 8, 2 * KB), 2)
    low = lane < KB
    for chunk in range(PAN // 32):
        start = chunk * 32
        acc = [None] * D
        for u in range(D):
            for q in range(PAIRS):
                y = y_ref[u * PAN + start : u * PAN + start + 32, q * 128 : (q + 1) * 128]
                y = y.reshape(4, 8, 128)
                for e in range(D):
                    term = y * mix_ref[column, (u * PAIRS + q) * D + e][None]
                    acc[e] = term if acc[e] is None else acc[e] + term
        for q in range(PAIRS):
            even, odd = acc[2 * q], acc[2 * q + 1]
            even = even + pltpu.roll(even.reshape(32, 128), KB, 1).reshape(4, 8, 128)
            odd = odd + pltpu.roll(odd.reshape(32, 128), KB, 1).reshape(4, 8, 128)
            both = jnp.where(low, even, odd).reshape(32, 128)
            res_ref[start : start + 32, q * 128 : (q + 1) * 128] = both.astype(jnp.bfloat16)


def turn_kernel(
    panels, odd_first, count,
    flag_ref, left_ref, low_ref, mid_ref, high_ref, ca_ref, cb_ref, mix_ref,
    keep_ref, send_ref, pass_ref,
    src, ya, yb, wide, res_a, res_b,
):
    s = pl.program_id(0)
    is_odd_home = flag_ref[0]
    is_first = flag_ref[1]
    even_total = panels + 2
    dump = 2 * panels + 6

    @pl.when(s == 0)
    def _():
        @pl.when(is_first == 1)
        def _():
            src[0 : panels + 4] = left_ref[0]

        @pl.when(is_first == 0)
        def _():
            src[0:2] = low_ref[...]
            src[2 : panels + 2] = mid_ref[...]
            src[panels + 2 : panels + 4] = high_ref[...]

        src[panels + 4 :] = jnp.zeros((panels + 3, PAN, LANES), jnp.bfloat16)
        yb[...] = jnp.zeros_like(yb)
        for column in range(2):
            for i in range(TERMS):
                wide[column, i] = jnp.broadcast_to(mix_ref[0, column, i : i + 1, :], (8, 128))

    def window(n):
        odd = jnp.clip(n - odd_first, 0, panels - 1) + panels + 4
        base = jnp.where(n < odd_first, jnp.minimum(n, panels + 1), odd)
        return src[pl.ds(base, 3)].reshape(BAND, LANES)

    def hand_out(n, res):
        slot = jnp.where((n >= 0) & (n < even_total), panels + 4 + n, dump)
        src[pl.ds(slot, 1)] = res[...][None]
        own_even = (n >= 1) & (n <= panels)
        own_odd = (n >= odd_first) & (n < odd_first + panels)
        to_keep = jnp.where(is_odd_home == 1, own_odd, own_even)
        to_send = jnp.where(is_odd_home == 1, own_even, own_odd)
        at_even = jnp.clip(n - 1, 0, panels - 1)
        at_odd = jnp.clip(n - odd_first, 0, panels - 1)
        at = jnp.where(own_odd, at_odd, at_even)

        @pl.when(to_keep)
        def _():
            keep_ref[pl.ds(at, 1)] = res[...][None]

        @pl.when(to_send)
        def _():
            send_ref[pl.ds(at, 1)] = res[...][None]

        @pl.when(own_odd)
        def _():
            pass_ref[pl.ds(at, 1)] = res[...][None]

    def phase(n):
        return (n >= odd_first).astype(jnp.int32)

    n = 2 * s

    @pl.when(s < count // 2)
    def _():
        ya[...] = jnp.dot(ca_ref[0], window(n), preferred_element_type=jnp.float32)
        mix_rows(yb, wide, phase(n - 1), res_b)
        hand_out(n - 1, res_b)
        yb[...] = jnp.dot(cb_ref[0], window(n + 1), preferred_element_type=jnp.float32)
        mix_rows(ya, wide, phase(n), res_a)
        hand_out(n, res_a)

    @pl.when(s == count // 2)
    def _():
        mix_rows(yb, wide, phase(n - 1), res_b)
        hand_out(n - 1, res_b)


def one_turn(flags, left, low, mid, high, bands, mixing):
    panels = mid.shape[0]
    gap = 0 if panels >= 2 else 1
    odd_first = panels + 2 + gap
    count = odd_first + panels
    count += count % 2
    last = 2 * panels + 1

    def band_at(n):
        return jnp.minimum(jnp.where(n < odd_first, jnp.minimum(n, panels + 1), n - gap), last)

    block = jax.ShapeDtypeStruct((panels, PAN, LANES), jnp.bfloat16)
    whole = lambda shape: pl.BlockSpec(shape, lambda s, f: (0,) * len(shape))
    spec = pltpu.PrefetchScalarGridSpec(
        num_scalar_prefetch=1,
        grid=(count // 2 + 1,),
        in_specs=[
            pl.BlockSpec((1, panels + 4, PAN, LANES), lambda s, f: (f[2], 0, 0, 0)),
            whole((2, PAN, LANES)),
            whole((panels, PAN, LANES)),
            whole((2, PAN, LANES)),
            pl.BlockSpec((1, STACK, BAND), lambda s, f: (band_at(2 * s), 0, 0)),
            pl.BlockSpec((1, STACK, BAND), lambda s, f: (band_at(2 * s + 1), 0, 0)),
            pl.BlockSpec((1, 2, TERMS, 128), lambda s, f: (f[2], 0, 0, 0)),
        ],
        out_specs=[whole((panels, PAN, LANES))] * 3,
        scratch_shapes=[
            pltpu.VMEM((2 * panels + 7, PAN, LANES), jnp.bfloat16),
            pltpu.VMEM((STACK, LANES), jnp.float32),
            pltpu.VMEM((STACK, LANES), jnp.float32),
            pltpu.VMEM((2, TERMS, 8, 128), jnp.float32),
            pltpu.VMEM((PAN, LANES), jnp.bfloat16),
            pltpu.VMEM((PAN, LANES), jnp.bfloat16),
        ],
    )
    steps = 2 * panels + 2
    return pl.pallas_call(
        functools.partial(turn_kernel, panels, odd_first, count),
        grid_spec=spec,
        out_shape=[block] * 3,
        compiler_params=pltpu.CompilerParams(vmem_limit_bytes=40 * MIB),
        cost_estimate=pl.CostEstimate(
            flops=steps * 2 * STACK * BAND * LANES * 2,
            bytes_accessed=steps * STACK * BAND * 2 * 3,
            transcendentals=0,
        ),
        name="two_columns",
    )(flags, left, low, mid, high, bands, bands, mixing)


def unpack_kernel(at_ref, held_ref, one_ref, two_ref, out_ref):
    rows = one_ref.shape[1]
    low = lax.broadcasted_iota(jnp.int32, (rows, 128), 1) < KB
    for q in range(PAIRS):
        one = one_ref[0, :, q * 128 : (q + 1) * 128].astype(jnp.float32)
        two = two_ref[0, :, q * 128 : (q + 1) * 128].astype(jnp.float32)
        first = jnp.where(low, one, pltpu.roll(two, KB, 1))
        second = jnp.where(low, pltpu.roll(one, KB, 1), two)
        out_ref[2 * q] = first.astype(jnp.bfloat16)
        out_ref[2 * q + 1] = second.astype(jnp.bfloat16)


def unpacked(at, held, one, two):
    panels = one.shape[0]
    return pl.pallas_call(
        unpack_kernel,
        grid_spec=pltpu.PrefetchScalarGridSpec(
            num_scalar_prefetch=1,
            grid=(panels,),
            in_specs=[
                pl.BlockSpec(memory_space=pl.ANY),
                pl.BlockSpec((1, PAN, LANES), lambda p, f: (p, 0, 0)),
                pl.BlockSpec((1, PAN, LANES), lambda p, f: (p, 0, 0)),
            ],
            out_specs=pl.BlockSpec((D, PAN, 128), lambda p, f: (0, p, f[0])),
        ),
        out_shape=jax.ShapeDtypeStruct(held.shape, held.dtype),
        input_output_aliases={1: 0},
        compiler_params=pltpu.CompilerParams(vmem_limit_bytes=32 * MIB),
        name="unpack",
    )(at, held, one, two)


def edges(block, width, axis_dim=0):
    count = lax.axis_size("sec")
    have = block.shape[axis_dim]
    low_parts, high_parts = [], []
    reach = 0
    while width > reach:
        hop = reach // have + 1
        take = min(have, width - reach)
        forward = [(i, i + hop) for i in range(count - hop)]
        backward = [(i + hop, i) for i in range(count - hop)]
        top = lax.slice_in_dim(block, have - take, have, axis=axis_dim)
        bottom = lax.slice_in_dim(block, 0, take, axis=axis_dim)
        low_parts.insert(0, lax.ppermute(top, "sec", forward))
        high_parts.append(lax.ppermute(bottom, "sec", backward))
        reach += take
    if len(low_parts) == 1:
        return low_parts[0], high_parts[0]
    return jnp.concatenate(low_parts, axis_dim), jnp.concatenate(high_parts, axis_dim)


def on_device(left_start, coupling, tensor, sketch, block_parity, leg_parity):
    row_count, _, rank = left_start.shape
    panels = row_count // PAN
    col_count = lax.axis_size("col")
    sec_count = lax.axis_size("sec")
    col_index = lax.axis_index("col")
    sec_index = lax.axis_index("sec")
    stage = col_index // 2
    half = col_index % 2
    stages = col_count // 2
    half_cols = rank // 2
    blocks = half_cols // KB
    swap = [(i, i ^ 1) for i in range(col_count)]
    up = [(i, i + 2) for i in range(col_count - 2)]

    legs = lax.dynamic_index_in_dim(leg_parity, col_index, 0, keepdims=False)
    parity = lax.dynamic_slice_in_dim(
        jnp.pad(block_parity, (1, 1)), sec_index * panels, panels + 2, 0
    )
    table = 1.0 - 2.0 * (parity[:, None] * legs[None, :]).astype(jnp.float32)
    signs = jnp.stack([table[w : w + panels] for w in range(3)], 1).reshape(panels, 3 * D)
    own = ordered_coupling(coupling[0], signs)
    other = lax.ppermute(own, "col", swap)
    own_low, own_high = edges(own, 1)
    other_low, other_high = edges(other, 1)
    odd_home = half == 1
    even_bands = [
        jnp.where(odd_home, b, a)
        for a, b in ((own_low, other_low), (own, other), (own_high, other_high))
    ]
    bands = jnp.concatenate(even_bands + [jnp.where(odd_home, own, other)], 0)

    small = jnp.concatenate([tensor[0].reshape(D, D * D * D), sketch[0]], 1)
    small_other = lax.ppermute(small, "col", swap)

    def mixing_of(both):
        legs_part = both[:, : D * D * D].reshape(D, D, D, D)
        cols = lax.dynamic_slice_in_dim(both, D * D * D + half * half_cols, half_cols, 1)
        m = jnp.einsum("duez,zk->duek", legs_part, cols, precision=lax.Precision.HIGHEST)
        m = m.reshape(PAIRS, 2, D, D, blocks, KB).transpose(4, 2, 0, 3, 1, 5)
        return m.reshape(blocks, TERMS, 2 * KB)

    mixing = jnp.stack(
        [
            mixing_of(jnp.where(odd_home, small_other, small)),
            mixing_of(jnp.where(odd_home, small, small_other)),
        ],
        1,
    )

    mine = lax.dynamic_slice_in_dim(left_start, half * half_cols, half_cols, 2)
    mine = mine.reshape(panels, PAN, PAIRS, 2, blocks, KB).transpose(4, 0, 1, 2, 3, 5)
    mine = mine.reshape(blocks, panels, PAN, LANES)
    left_low, left_high = edges(mine, 2, 1)
    left = jnp.concatenate([left_low, mine, left_high], 1)

    skew = 2
    turns = blocks + skew * (stages - 1)
    zero_edge = jnp.zeros((2, PAN, LANES), jnp.bfloat16)
    zero_mid = jnp.zeros((panels, PAN, LANES), jnp.bfloat16)
    arrived = {t: (zero_edge, zero_mid, zero_edge) for t in range(skew)}
    keeps, sends = {}, {}
    kept, got = [], []
    lag = skew * (stages - 1)
    states = jnp.zeros((D, row_count, rank), jnp.bfloat16)

    def staged(table_of, i):
        out = table_of[i + lag]
        for z in range(stages - 1):
            out = jnp.where(stage == z, table_of[i + skew * z], out)
        return out

    for t in range(turns):
        index = jnp.clip(t - skew * stage, 0, blocks - 1)
        flags = jnp.stack([half, (stage == 0).astype(jnp.int32), index]).astype(jnp.int32)
        low, mid, high = arrived.pop(t)
        keeps[t], sends[t], passed = one_turn(flags, left, low, mid, high, bands, mixing)
        if t + skew < turns:
            nxt = lax.ppermute(passed, "col", up)
            nlow, nhigh = edges(nxt, 2)
            arrived[t + skew] = (nlow, nxt, nhigh)
        if t >= lag:
            i = t - lag
            got.append(lax.ppermute(staged(sends, i), "col", swap))
            kept.append(staged(keeps, i))
            if i % 2 == 1:
                at_own = (half * (blocks // 2) + i // 2).astype(jnp.int32)[None]
                at_got = ((1 - half) * (blocks // 2) + i // 2).astype(jnp.int32)[None]
                states = unpacked(at_own, states, kept[i - 1], kept[i])
                states = unpacked(at_got, states, got[i - 1], got[i])

    flat = states.reshape(D * row_count, rank)
    partial = lax.dot_general(
        flat, flat, (((0,), (0,)), ((), ())), preferred_element_type=jnp.float32
    ).astype(jnp.bfloat16)
    share = rank // sec_count
    gram = partial.reshape(sec_count, share, rank)
    width = 1
    while width < sec_count:
        bit = (sec_index // width) % 2
        pairs = gram.reshape(-1, 2, share, rank)
        stay = lax.dynamic_index_in_dim(pairs, bit, 1, keepdims=False)
        away = lax.dynamic_index_in_dim(pairs, 1 - bit, 1, keepdims=False)
        come = lax.ppermute(away, "sec", [(i, i ^ width) for i in range(sec_count)])
        gram = stay.astype(jnp.float32) + come.astype(jnp.float32)
        if gram.shape[0] > 1:
            gram = gram.astype(jnp.bfloat16)
        width *= 2
    gram_out = gram * (1.0 / (CHI * D))
    return states.transpose(1, 0, 2)[None], gram_out


def solution(mesh):
    in_specs = (
        P("sec", None, None),
        P("col", "sec", None),
        P("col", None, None, None, None),
        P("col", None, None),
        P(),
        P(),
    )
    out_specs = (P("col", "sec", None, None), P("col", "sec", None))
    return jax.shard_map(
        on_device, mesh=mesh, in_specs=in_specs, out_specs=out_specs, check_vma=False
    )
```

time: 1930 us -> 511 us (0.26)
  local copies, waits for them, and re-layouts: 916 us -> 54.2 us
  matrix products: 357 us -> 12.9 us
  Pallas kernels: 0 us -> 197 us
  waiting for transfers between devices: 270 us -> 81.3 us
  other arithmetic: 200 us -> 19.7 us
  starting transfers between devices: 155 us -> 134 us
    dot_general x62 -> x3, matrix products: 357 us -> 12.9 us  [the longest x1 10.7 us: on_device(): lax.dot_general(flat, flat, (((0,), (0,)), ((), ())), preferred_element_t...]
    transpose x15 -> x1, local copies, waits for them, and re-layouts: 283 us -> 4.4 us  [on_device(): mine.reshape(panels, PAN, PAIRS, 2, blocks, KB).transpose(4, 0, 1, 2, 3, 5)]
    reshape x30 -> x3, local copies, waits for them, and re-layouts: 275 us -> 10.2 us  [the longest x1 5.49 us: on_device(): mine.reshape(panels, PAN, PAIRS, 2, blocks, KB).transpose(4, 0, 1, 2, 3, 5)]
    slice x75 -> x17, local copies, waits for them, and re-layouts: 268 us -> 7.1 us  [the longest x3 6.6 us: edges(): top = lax.slice_in_dim(block, have - take, have, axis=axis_dim)]
    pallas_call x0 -> x23, Pallas kernels: none -> 197 us  [the longest x14 174 us: one_turn(): pl.pallas_call(functools.partial(turn_kernel, panels, odd_first, count),...]
    ppermute x45 -> x54, waiting for transfers between devices: 224 us -> 81.3 us  [the longest x8 29.5 us: on_device(): got.append(lax.ppermute(staged(sends, i), 'col', swap))]
    convert_element_type x16 -> x2, other arithmetic: 145 us -> 2.73 us  [the longest x1 1.64 us: on_device(): gram = gram.astype(jnp.bfloat16)]
    dynamic_slice x60 -> x3, local copies, waits for them, and re-layouts: 62.9 us -> 9.31 us  [the longest x2 8.58 us: on_device(): mine = lax.dynamic_slice_in_dim(left_start, half * half_cols, half_cols, 2)]
  transfers between devices with their start and end apart: 46 -> 54, of which waited for: 16 -> 14; matrix products, arithmetic and copies ran while one was open for 4% -> 11% of each run, Pallas kernels for 0% -> 35%
where the time goes in v1:
time: 511 us; the launch traced here: 501 us
  Pallas kernels  197 us (39%)
  starting transfers between devices  134 us (26%)
  waiting for transfers between devices  81.3 us (16%)
  local copies, waits for them, and re-layouts  54.2 us (11%)
  other arithmetic  19.7 us (4%)
  matrix products  12.9 us (3%)
    pallas_call x14, Pallas kernels, one_turn(): pl.pallas_call(functools.partial(turn_kernel, panels, odd_first, count),...  174 us
    ppermute x15, starting transfers between devices, edges(): low_parts.insert(0, lax.ppermute(top, 'sec', forward))  56.9 us
    ppermute x12, starting transfers between devices, on_device(): nxt = lax.ppermute(passed, 'col', up)  39 us
    ppermute x8, waiting for transfers between devices, on_device(): got.append(lax.ppermute(staged(sends, i), 'col', swap))  29.5 us
    ppermute x12, waiting for transfers between devices, on_device(): nxt = lax.ppermute(passed, 'col', up)  23.2 us
    ppermute x15, starting transfers between devices, edges(): high_parts.append(lax.ppermute(bottom, 'sec', backward))  19.7 us
    pallas_call x8, Pallas kernels, unpacked(): pl.pallas_call(unpack_kernel, grid_spec=pltpu.PrefetchScalarGridSpec(num_...  17.3 us
    ppermute x2, waiting for transfers between devices, on_device(): come = lax.ppermute(away, 'sec', [(i, i ^ width) for i in range(sec_count)])  14.6 us
  transfers between devices with their start and end apart: 54, of which 14 were waited for; matrix products, arithmetic and copies ran while one was open for 11% of the time, Pallas kernels for 35%

profile of v1, /device:TPU:0, one launch (start us, length us, event | category | flops | bytes accessed | tf_op | source)
XLA Modules:
  0.0 501.5 jit_solution(5320013125485456325)
XLA Ops:
  5.0 5.3 %order_coupling.1 = bf16[4,768,384]{2,1,0:T(8,128)(2,1)S(1)} custom-call(f32[4,18]{1,0:T(4,128)S(1)} %reshape.36.sign_ref, bf16[512,2304]{1,0:T(8,128)(2,1)S(1)} %bitcast.75, bf16[768,768]{1,0:T(8,128)(2,1)S(1)} %fusion.perm_ref), custom_call_target="tpu_custom_call" | custom-call | tf_op jit(solution)/shard_map/order_coupling/pallas_call | solution.py:39
  23.6 4.6 copy.21
  28.2 5.5 %reshape.34 = bf16[4,128,3,2,8,64]{1,0,5,4,3,2:T(4,128)(2,1)} reshape(bf16[512,6,512]{0,2,1:T(8,128)(2,1)} %copy.21) | data formatting | bytes 6291456 | tf_op jit(solution)/shard_map/reshape | solution.py:307
  38.1 4.6 copy.23
  51.6 13.9 %collective-permute-done.7 = f32[6,1240]{1,0:T(8,128)S(1)} collective-permute-done((f32[6,1240]{1,0:T(8,128)S(1)}, f32[6,1240]{1,0:T(8,128)S(1)}, u32[]{:S(2)}, u32[]{:S(2)}) %collective-permute-start.7) | collective-permute-done | bytes 29792 | tf_op jit(solution)/shard_map/ppermute | solution.py:289
  78.6 5.1 %pad_maximum_fusion.left_ref = bf16[8,8,128,384]{3,2,1,0:T(8,128)(2,1)} fusion(bf16[8,2,128,384]{3,2,1,0:T(8,128)(2,1)} %collective-permute-done.1, bf16[8,4,128,384]{3,2,1,0:T(8,128)(2,1)S(1)} %copy-done.43, bf16[8,2,128,384]{3,2,1,0:T(8,128)(2,1)} %collective-permute-done), kind=kLoop, calls=%fused_computation | loop fusion | flops 6291456 | bytes 12582912 | tf_op jit(solution)/shard_map/concatenate | solution.py:310
  83.7 11.2 %collective-permute-start.3 = (bf16[1,768,384]{2,1,0:T(8,128)(2,1)S(1)}, bf16[1,768,384]{2,1,0:T(8,128)(2,1)S(1)}, u32[]{:S(2)}, u32[]{:S(2)}) collective-permute-start(bf16[1,768,384]{2,1,0:T(8,128)(2,1)S(1)} %get-tuple-element.90), channel_id=1, source_target_pairs={{0,1},{1,2},{2,3},{4,5},{5,6},{6,7},{8,9},{9,10},{10,11},{12,13},{... | collective-permute-start | bytes 1769480 | tf_op jit(solution)/shard_map/ppermute | solution.py:248
  100.3 12.8 %two_columns.18 = (bf16[4,128,384]{2,1,0:T(8,128)(2,1)S(1)}, bf16[4,128,384]{2,1,0:T(8,128)(2,1)S(1)}, bf16[4,128,384]{2,1,0:T(8,128)(2,1)S(1)}) custom-call(s32[3]{0:T(128)S(1)} %get-tuple-element.143.flag_ref, bf16[8,8,128,384]{3,2,1,0:T(8,128)(2,1)} %pad_maximum_fusion.left_ref, bf16[2,128,384]{2,1,0:T(8,128)(2,1)S(1)} %broadcast_in_dim.47.low_ref.high_ref, ...), custom_call_target="tpu_custom_call" | custom-call | flops 4529848320 | bytes 17694720 | tf_op jit(solution)/shard_map/two_columns/pallas_call | solution.py:189
  117.4 12.2 %two_columns.14 = (bf16[4,128,384]{2,1,0:T(8,128)(2,1)S(1)}, bf16[4,128,384]{2,1,0:T(8,128)(2,1)S(1)}, bf16[4,128,384]{2,1,0:T(8,128)(2,1)S(1)}) custom-call(s32[3]{0:T(128)S(1)} %get-tuple-element.147.flag_ref, bf16[8,8,128,384]{3,2,1,0:T(8,128)(2,1)} %pad_maximum_fusion.left_ref, bf16[2,128,384]{2,1,0:T(8,128)(2,1)S(1)} %broadcast_in_dim.47.low_ref.high_ref, ...), custom_call_target="tpu_custom_call" | custom-call | flops 4529848320 | bytes 17694720 | tf_op jit(solution)/shard_map/two_columns/pallas_call | solution.py:189
  142.6 4.8 collective-permute-start.9
  147.4 12.2 %two_columns.19 = (bf16[4,128,384]{2,1,0:T(8,128)(2,1)S(1)}, bf16[4,128,384]{2,1,0:T(8,128)(2,1)S(1)}, bf16[4,128,384]{2,1,0:T(8,128)(2,1)S(1)}) custom-call(s32[3]{0:T(128)S(1)} %get-tuple-element.144.flag_ref, bf16[8,8,128,384]{3,2,1,0:T(8,128)(2,1)} %pad_maximum_fusion.left_ref, bf16[2,128,384]{2,1,0:T(8,128)(2,1)S(1)} %collective-permute-done.18.low_ref, ...), custom_call_target="tpu_custom_call" | custom-call | flops 4529848320 | bytes 17694720 | tf_op jit(solution)/shard_map/two_columns/pallas_call | solution.py:189
  164.9 12.2 %two_columns.15 = (bf16[4,128,384]{2,1,0:T(8,128)(2,1)S(1)}, bf16[4,128,384]{2,1,0:T(8,128)(2,1)S(1)}, bf16[4,128,384]{2,1,0:T(8,128)(2,1)S(1)}) custom-call(s32[3]{0:T(128)S(1)} %get-tuple-element.148.flag_ref, bf16[8,8,128,384]{3,2,1,0:T(8,128)(2,1)} %pad_maximum_fusion.left_ref, bf16[2,128,384]{2,1,0:T(8,128)(2,1)S(1)} %collective-permute-done.9.low_ref, ...), custom_call_target="tpu_custom_call" | custom-call | flops 4529848320 | bytes 17694720 | tf_op jit(solution)/shard_map/two_columns/pallas_call | solution.py:189
  185.0 4.6 collective-permute-done.11.mid_ref
  193.5 12.2 %two_columns.20 = (bf16[4,128,384]{2,1,0:T(8,128)(2,1)S(1)}, bf16[4,128,384]{2,1,0:T(8,128)(2,1)S(1)}, bf16[4,128,384]{2,1,0:T(8,128)(2,1)S(1)}) custom-call(s32[3]{0:T(128)S(1)} %get-tuple-element.145.flag_ref, bf16[8,8,128,384]{3,2,1,0:T(8,128)(2,1)} %pad_maximum_fusion.left_ref, bf16[2,128,384]{2,1,0:T(8,128)(2,1)S(1)} %collective-permute-done.21.low_ref, ...), custom_call_target="tpu_custom_call" | custom-call | flops 4529848320 | bytes 17694720 | tf_op jit(solution)/shard_map/two_columns/pallas_call | solution.py:189
  210.5 12.2 %two_columns.16 = (bf16[4,128,384]{2,1,0:T(8,128)(2,1)S(1)}, bf16[4,128,384]{2,1,0:T(8,128)(2,1)S(1)}, bf16[4,128,384]{2,1,0:T(8,128)(2,1)S(1)}) custom-call(s32[3]{0:T(128)S(1)} %get-tuple-element.149.flag_ref, bf16[8,8,128,384]{3,2,1,0:T(8,128)(2,1)} %pad_maximum_fusion.left_ref, bf16[2,128,384]{2,1,0:T(8,128)(2,1)S(1)} %collective-permute-done.12.low_ref, ...), custom_call_target="tpu_custom_call" | custom-call | flops 4529848320 | bytes 17694720 | tf_op jit(solution)/shard_map/two_columns/pallas_call | solution.py:189
  228.9 5.1 %collective-permute-done.14.mid_ref = bf16[4,128,384]{2,1,0:T(8,128)(2,1)S(1)} collective-permute-done((bf16[4,128,384]{2,1,0:T(8,128)(2,1)S(1)}, bf16[4,128,384]{2,1,0:T(8,128)(2,1)S(1)}, u32[]{:S(2)}, u32[]{:S(2)}) %collective-permute-start.14) | collective-permute-done | bytes 393248 | tf_op jit(solution)/shard_map/ppermute | solution.py:334
  237.8 12.2 %two_columns.21 = (bf16[4,128,384]{2,1,0:T(8,128)(2,1)S(1)}, bf16[4,128,384]{2,1,0:T(8,128)(2,1)S(1)}, bf16[4,128,384]{2,1,0:T(8,128)(2,1)S(1)}) custom-call(s32[3]{0:T(128)S(1)} %get-tuple-element.142.flag_ref, bf16[8,8,128,384]{3,2,1,0:T(8,128)(2,1)} %pad_maximum_fusion.left_ref, bf16[2,128,384]{2,1,0:T(8,128)(2,1)S(1)} %collective-permute-done.24.low_ref, ...), custom_call_target="tpu_custom_call" | custom-call | flops 4529848320 | bytes 17694720 | tf_op jit(solution)/shard_map/two_columns/pallas_call | solution.py:189
  255.0 12.2 %two_columns.17 = (bf16[4,128,384]{2,1,0:T(8,128)(2,1)S(1)}, bf16[4,128,384]{2,1,0:T(8,128)(2,1)S(1)}, bf16[4,128,384]{2,1,0:T(8,128)(2,1)S(1)}) custom-call(s32[3]{0:T(128)S(1)} %get-tuple-element.146.flag_ref, bf16[8,8,128,384]{3,2,1,0:T(8,128)(2,1)} %pad_maximum_fusion.left_ref, bf16[2,128,384]{2,1,0:T(8,128)(2,1)S(1)} %collective-permute-done.15.low_ref, ...), custom_call_target="tpu_custom_call" | custom-call | flops 4529848320 | bytes 17694720 | tf_op jit(solution)/shard_map/two_columns/pallas_call | solution.py:189
  273.6 4.7 collective-permute-done.28.mid_ref
  282.1 12.2 %two_columns.23 = (bf16[4,128,384]{2,1,0:T(8,128)(2,1)S(1)}, bf16[4,128,384]{2,1,0:T(8,128)(2,1)S(1)}, bf16[4,128,384]{2,1,0:T(8,128)(2,1)S(1)}) custom-call(s32[3]{0:T(128)S(1)} %get-tuple-element.140.flag_ref, bf16[8,8,128,384]{3,2,1,0:T(8,128)(2,1)} %pad_maximum_fusion.left_ref, bf16[2,128,384]{2,1,0:T(8,128)(2,1)S(1)} %collective-permute-done.32.low_ref, ...), custom_call_target="tpu_custom_call" | custom-call | flops 4529848320 | bytes 17694720 | tf_op jit(solution)/shard_map/two_columns/pallas_call | solution.py:189
  299.2 12.2 %two_columns.22 = (bf16[4,128,384]{2,1,0:T(8,128)(2,1)S(1)}, bf16[4,128,384]{2,1,0:T(8,128)(2,1)S(1)}, bf16[4,128,384]{2,1,0:T(8,128)(2,1)S(1)}) custom-call(s32[3]{0:T(128)S(1)} %get-tuple-element.141.flag_ref, bf16[8,8,128,384]{3,2,1,0:T(8,128)(2,1)} %pad_maximum_fusion.left_ref, bf16[2,128,384]{2,1,0:T(8,128)(2,1)S(1)} %collective-permute-done.29.low_ref, ...), custom_call_target="tpu_custom_call" | custom-call | flops 4529848320 | bytes 17694720 | tf_op jit(solution)/shard_map/two_columns/pallas_call | solution.py:189
  326.2 13.0 %two_columns.25 = (bf16[4,128,384]{2,1,0:T(8,128)(2,1)S(1)}, bf16[4,128,384]{2,1,0:T(8,128)(2,1)S(1)}, bf16[4,128,384]{2,1,0:T(8,128)(2,1)}) custom-call(s32[3]{0:T(128)S(1)} %get-tuple-element.138.flag_ref, bf16[8,8,128,384]{3,2,1,0:T(8,128)(2,1)} %pad_maximum_fusion.left_ref, bf16[2,128,384]{2,1,0:T(8,128)(2,1)S(1)} %collective-permute-done.40.low_ref, ...), custom_call_target="tpu_custom_call" | custom-call | flops 4529848320 | bytes 17694720 | tf_op jit(solution)/shard_map/two_columns/pallas_call | solution.py:189
  344.1 13.0 %two_columns.24 = (bf16[4,128,384]{2,1,0:T(8,128)(2,1)S(1)}, bf16[4,128,384]{2,1,0:T(8,128)(2,1)S(1)}, bf16[4,128,384]{2,1,0:T(8,128)(2,1)}) custom-call(s32[3]{0:T(128)S(1)} %get-tuple-element.139.flag_ref, bf16[8,8,128,384]{3,2,1,0:T(8,128)(2,1)} %pad_maximum_fusion.left_ref, bf16[2,128,384]{2,1,0:T(8,128)(2,1)S(1)} %collective-permute-done.37.low_ref, ...), custom_call_target="tpu_custom_call" | custom-call | flops 4529848320 | bytes 17694720 | tf_op jit(solution)/shard_map/two_columns/pallas_call | solution.py:189
  376.4 12.9 %two_columns.27 = (bf16[4,128,384]{2,1,0:T(8,128)(2,1)S(1)}, bf16[4,128,384]{2,1,0:T(8,128)(2,1)S(1)}, bf16[4,128,384]{2,1,0:T(8,128)(2,1)}) custom-call(s32[3]{0:T(128)S(1)} %get-tuple-element.82.flag_ref, bf16[8,8,128,384]{3,2,1,0:T(8,128)(2,1)} %pad_maximum_fusion.left_ref, bf16[2,128,384]{2,1,0:T(8,128)(2,1)S(1)} %collective-permute-done.48.low_ref, ...), custom_call_target="tpu_custom_call" | custom-call | flops 4529848320 | bytes 17694720 | tf_op jit(solution)/shard_map/two_columns/pallas_call | solution.py:189
  390.8 12.9 %two_columns.26 = (bf16[4,128,384]{2,1,0:T(8,128)(2,1)S(1)}, bf16[4,128,384]{2,1,0:T(8,128)(2,1)S(1)}, bf16[4,128,384]{2,1,0:T(8,128)(2,1)}) custom-call(s32[3]{0:T(128)S(1)} %get-tuple-element.137.flag_ref, bf16[8,8,128,384]{3,2,1,0:T(8,128)(2,1)} %pad_maximum_fusion.left_ref, bf16[2,128,384]{2,1,0:T(8,128)(2,1)S(1)} %collective-permute-done.45.low_ref, ...), custom_call_target="tpu_custom_call" | custom-call | flops 4529848320 | bytes 17694720 | tf_op jit(solution)/shard_map/two_columns/pallas_call | solution.py:189
  412.0 4.9 collective-permute-done.26.one_ref
  419.3 5.9 %collective-permute-done.35.two_ref = bf16[4,128,384]{2,1,0:T(8,128)(2,1)} collective-permute-done((bf16[4,128,384]{2,1,0:T(8,128)(2,1)}, bf16[4,128,384]{2,1,0:T(8,128)(2,1)}, u32[]{:S(2)}, u32[]{:S(2)}) %collective-permute-start.35) | collective-permute-done | bytes 393248 | tf_op jit(solution)/shard_map/ppermute | solution.py:339
  445.3 5.3 %collective-permute-done.42.one_ref = bf16[4,128,384]{2,1,0:T(8,128)(2,1)S(1)} collective-permute-done((bf16[4,128,384]{2,1,0:T(8,128)(2,1)}, bf16[4,128,384]{2,1,0:T(8,128)(2,1)S(1)}, u32[]{:S(2)}, u32[]{:S(2)}) %collective-permute-start.42) | collective-permute-done | bytes 393248 | tf_op jit(solution)/shard_map/ppermute | solution.py:339
  454.1 4.9 collective-permute-done.51.two_ref
  459.0 8.4 %collective-permute-done.50.one_ref = bf16[4,128,384]{2,1,0:T(8,128)(2,1)S(1)} collective-permute-done((bf16[4,128,384]{2,1,0:T(8,128)(2,1)}, bf16[4,128,384]{2,1,0:T(8,128)(2,1)S(1)}, u32[]{:S(2)}, u32[]{:S(2)}) %collective-permute-start.50) | collective-permute-done | bytes 393248 | tf_op jit(solution)/shard_map/ppermute | solution.py:339
  469.2 10.7 %bitcast_convert_fusion = bf16[1024,1024]{1,0:T(8,128)(2,1)S(1)} fusion(bf16[6,512,1024]{2,1,0:T(8,128)(2,1)} %unpack.15), kind=kOutput, calls=%fused_computation.2 | convolution fusion | flops 6443499520 | bytes 8388608 | tf_op jit(solution)/shard_map/dot_general | solution.py:348
  487.7 12.2 %collective-permute-done.53 = bf16[1,256,1024]{2,1,0:T(8,128)(2,1)S(1)} collective-permute-done((bf16[1,256,1024]{2,1,0:T(8,128)(2,1)S(1)}, bf16[1,256,1024]{2,1,0:T(8,128)(2,1)S(1)}, u32[]{:S(2)}, u32[]{:S(2)}) %collective-permute-start.53) | collective-permute-done | bytes 524320 | tf_op jit(solution)/shard_map/ppermute | solution.py:359
  (265 shorter events, 202.7 us)
Async XLA Ops:
  10.3 65.6 %collective-permute-start.2 = (bf16[4,768,384]{2,1,0:T(8,128)(2,1)S(1)}, bf16[4,768,384]{2,1,0:T(8,128)(2,1)}, u32[]{:S(2)}, u32[]{:S(2)}) collective-permute-start(bf16[4,768,384]{2,1,0:T(8,128)(2,1)S(1)} %order_coupling.1), channel_id=1, source_target_pairs={{0,4},{4,0},{8,12},{12,8},{16,20},{20,16},{24,28},{28,24},{1,5},{5... | collective-permute-start | bytes 7077896 | tf_op jit(solution)/shard_map/ppermute | solution.py:278
  14.5 82.5 %collective-permute-start.6 = (bf16[1,768,384]{2,1,0:T(8,128)(2,1)}, bf16[1,768,384]{2,1,0:T(8,128)(2,1)}, u32[]{:S(2)}, u32[]{:S(2)}) collective-permute-start(bf16[1,768,384]{2,1,0:T(8,128)(2,1)} %get-tuple-element.89), channel_id=1, source_target_pairs={{1,0},{2,1},{3,2},{5,4},{6,5},{7,6},{9,8},{10,9},{11,10},{13,12},{... | collective-permute-start | bytes 1769480 | tf_op jit(solution)/shard_map/ppermute | solution.py:249
  15.8 82.4 %collective-permute-start.4 = (bf16[1,768,384]{2,1,0:T(8,128)(2,1)}, bf16[1,768,384]{2,1,0:T(8,128)(2,1)}, u32[]{:S(2)}, u32[]{:S(2)}) collective-permute-start(bf16[1,768,384]{2,1,0:T(8,128)(2,1)} %get-tuple-element.88), channel_id=1, source_target_pairs={{0,1},{1,2},{2,3},{4,5},{5,6},{6,7},{8,9},{9,10},{10,11},{12,13},{... | collective-permute-start | bytes 1769480 | tf_op jit(solution)/shard_map/ppermute | solution.py:248
  46.8 31.8 %collective-permute-start = (bf16[8,2,128,384]{3,2,1,0:T(8,128)(2,1)}, bf16[8,2,128,384]{3,2,1,0:T(8,128)(2,1)}, u32[]{:S(2)}, u32[]{:S(2)}) collective-permute-start(bf16[8,2,128,384]{3,2,1,0:T(8,128)(2,1)} %get-tuple-element.86), channel_id=1, source_target_pairs={{0,1},{1,2},{2,3},{4,5},{5,6},{6,7},{8,9},{9,10},{10,11},{12,13},{... | collective-permute-start | bytes 4718600 | tf_op jit(solution)/shard_map/ppermute | solution.py:248
  50.8 14.7 %collective-permute-start.7 = (f32[6,1240]{1,0:T(8,128)S(1)}, f32[6,1240]{1,0:T(8,128)S(1)}, u32[]{:S(2)}, u32[]{:S(2)}) collective-permute-start(f32[6,1240]{1,0:T(8,128)S(1)} %pad_maximum_fusion.2), channel_id=1, source_target_pairs={{0,4},{4,0},{8,12},{12,8},{16,20},{20,16},{24,28},{28,24},{1,5},{5... | collective-permute-start | bytes 89288 | tf_op jit(solution)/shard_map/ppermute | solution.py:289
  77.3 19.7 %collective-permute-start.5 = (bf16[1,768,384]{2,1,0:T(8,128)(2,1)S(1)}, bf16[1,768,384]{2,1,0:T(8,128)(2,1)S(1)}, u32[]{:S(2)}, u32[]{:S(2)}) collective-permute-start(bf16[1,768,384]{2,1,0:T(8,128)(2,1)S(1)} %get-tuple-element.91), channel_id=1, source_target_pairs={{1,0},{2,1},{3,2},{5,4},{6,5},{7,6},{9,8},{10,9},{11,10},{13,12},{... | collective-permute-start | bytes 1769480 | tf_op jit(solution)/shard_map/ppermute | solution.py:249
  113.9 19.9 %collective-permute-start.17 = (bf16[4,128,384]{2,1,0:T(8,128)(2,1)S(1)}, bf16[4,128,384]{2,1,0:T(8,128)(2,1)S(1)}, u32[]{:S(2)}, u32[]{:S(2)}) collective-permute-start(bf16[4,128,384]{2,1,0:T(8,128)(2,1)S(1)} %get-tuple-element.49), channel_id=1, source_target_pairs={{0,8},{4,12},{8,16},{12,20},{16,24},{20,28},{1,9},{5,13},{9,17},{1... | collective-permute-start | bytes 1179656 | tf_op jit(solution)/shard_map/ppermute | solution.py:334
  141.3 23.6 %collective-permute-start.10 = (bf16[2,128,384]{2,1,0:T(8,128)(2,1)S(1)}, bf16[2,128,384]{2,1,0:T(8,128)(2,1)S(1)}, u32[]{:S(2)}, u32[]{:S(2)}) collective-permute-start(bf16[2,128,384]{2,1,0:T(8,128)(2,1)S(1)} %get-tuple-element.130), channel_id=1, source_target_pairs={{1,0},{2,1},{3,2},{5,4},{6,5},{7,6},{9,8},{10,9},{11,10},{13,12},{... | collective-permute-start | bytes 589832 | tf_op jit(solution)/shard_map/ppermute | solution.py:249
  142.6 22.3 %collective-permute-start.9 = (bf16[2,128,384]{2,1,0:T(8,128)(2,1)S(1)}, bf16[2,128,384]{2,1,0:T(8,128)(2,1)S(1)}, u32[]{:S(2)}, u32[]{:S(2)}) collective-permute-start(bf16[2,128,384]{2,1,0:T(8,128)(2,1)S(1)} %get-tuple-element.131), channel_id=1, source_target_pairs={{0,1},{1,2},{2,3},{4,5},{5,6},{6,7},{8,9},{9,10},{10,11},{12,13},{... | collective-permute-start | bytes 589832 | tf_op jit(solution)/shard_map/ppermute | solution.py:248
  160.4 20.2 %collective-permute-start.20 = (bf16[4,128,384]{2,1,0:T(8,128)(2,1)S(1)}, bf16[4,128,384]{2,1,0:T(8,128)(2,1)S(1)}, u32[]{:S(2)}, u32[]{:S(2)}) collective-permute-start(bf16[4,128,384]{2,1,0:T(8,128)(2,1)S(1)} %get-tuple-element.50), channel_id=1, source_target_pairs={{0,8},{4,12},{8,16},{12,20},{16,24},{20,28},{1,9},{5,13},{9,17},{1... | collective-permute-start | bytes 1179656 | tf_op jit(solution)/shard_map/ppermute | solution.py:334
  189.7 20.8 %collective-permute-start.12 = (bf16[2,128,384]{2,1,0:T(8,128)(2,1)S(1)}, bf16[2,128,384]{2,1,0:T(8,128)(2,1)S(1)}, u32[]{:S(2)}, u32[]{:S(2)}) collective-permute-start(bf16[2,128,384]{2,1,0:T(8,128)(2,1)S(1)} %get-tuple-element.129), channel_id=1, source_target_pairs={{0,1},{1,2},{2,3},{4,5},{5,6},{6,7},{8,9},{9,10},{10,11},{12,13},{... | collective-permute-start | bytes 589832 | tf_op jit(solution)/shard_map/ppermute | solution.py:248
  192.1 18.4 %collective-permute-start.13 = (bf16[2,128,384]{2,1,0:T(8,128)(2,1)S(1)}, bf16[2,128,384]{2,1,0:T(8,128)(2,1)S(1)}, u32[]{:S(2)}, u32[]{:S(2)}) collective-permute-start(bf16[2,128,384]{2,1,0:T(8,128)(2,1)S(1)} %get-tuple-element.128), channel_id=1, source_target_pairs={{1,0},{2,1},{3,2},{5,4},{6,5},{7,6},{9,8},{10,9},{11,10},{13,12},{... | collective-permute-start | bytes 589832 | tf_op jit(solution)/shard_map/ppermute | solution.py:249
  206.4 18.3 %collective-permute-start.23 = (bf16[4,128,384]{2,1,0:T(8,128)(2,1)S(1)}, bf16[4,128,384]{2,1,0:T(8,128)(2,1)S(1)}, u32[]{:S(2)}, u32[]{:S(2)}) collective-permute-start(bf16[4,128,384]{2,1,0:T(8,128)(2,1)S(1)} %get-tuple-element.54), channel_id=1, source_target_pairs={{0,8},{4,12},{8,16},{12,20},{16,24},{20,28},{1,9},{5,13},{9,17},{1... | collective-permute-start | bytes 1179656 | tf_op jit(solution)/shard_map/ppermute | solution.py:334
  234.1 20.9 %collective-permute-start.15 = (bf16[2,128,384]{2,1,0:T(8,128)(2,1)S(1)}, bf16[2,128,384]{2,1,0:T(8,128)(2,1)S(1)}, u32[]{:S(2)}, u32[]{:S(2)}) collective-permute-start(bf16[2,128,384]{2,1,0:T(8,128)(2,1)S(1)} %get-tuple-element.127), channel_id=1, source_target_pairs={{0,1},{1,2},{2,3},{4,5},{5,6},{6,7},{8,9},{9,10},{10,11},{12,13},{... | collective-permute-start | bytes 589832 | tf_op jit(solution)/shard_map/ppermute | solution.py:248
  236.3 18.7 %collective-permute-start.16 = (bf16[2,128,384]{2,1,0:T(8,128)(2,1)S(1)}, bf16[2,128,384]{2,1,0:T(8,128)(2,1)S(1)}, u32[]{:S(2)}, u32[]{:S(2)}) collective-permute-start(bf16[2,128,384]{2,1,0:T(8,128)(2,1)S(1)} %get-tuple-element.126), channel_id=1, source_target_pairs={{1,0},{2,1},{3,2},{5,4},{6,5},{7,6},{9,8},{10,9},{11,10},{13,12},{... | collective-permute-start | bytes 589832 | tf_op jit(solution)/shard_map/ppermute | solution.py:249
  250.8 18.4 %collective-permute-start.31 = (bf16[4,128,384]{2,1,0:T(8,128)(2,1)S(1)}, bf16[4,128,384]{2,1,0:T(8,128)(2,1)S(1)}, u32[]{:S(2)}, u32[]{:S(2)}) collective-permute-start(bf16[4,128,384]{2,1,0:T(8,128)(2,1)S(1)} %get-tuple-element.66), channel_id=1, source_target_pairs={{0,8},{4,12},{8,16},{12,20},{16,24},{20,28},{1,9},{5,13},{9,17},{1... | collective-permute-start | bytes 1179656 | tf_op jit(solution)/shard_map/ppermute | solution.py:334
  278.4 20.8 %collective-permute-start.29 = (bf16[2,128,384]{2,1,0:T(8,128)(2,1)S(1)}, bf16[2,128,384]{2,1,0:T(8,128)(2,1)S(1)}, u32[]{:S(2)}, u32[]{:S(2)}) collective-permute-start(bf16[2,128,384]{2,1,0:T(8,128)(2,1)S(1)} %get-tuple-element.119), channel_id=1, source_target_pairs={{0,1},{1,2},{2,3},{4,5},{5,6},{6,7},{8,9},{9,10},{10,11},{12,13},{... | collective-permute-start | bytes 589832 | tf_op jit(solution)/shard_map/ppermute | solution.py:248
  280.7 18.4 %collective-permute-start.30 = (bf16[2,128,384]{2,1,0:T(8,128)(2,1)S(1)}, bf16[2,128,384]{2,1,0:T(8,128)(2,1)S(1)}, u32[]{:S(2)}, u32[]{:S(2)}) collective-permute-start(bf16[2,128,384]{2,1,0:T(8,128)(2,1)S(1)} %get-tuple-element.118), channel_id=1, source_target_pairs={{1,0},{2,1},{3,2},{5,4},{6,5},{7,6},{9,8},{10,9},{11,10},{13,12},{... | collective-permute-start | bytes 589832 | tf_op jit(solution)/shard_map/ppermute | solution.py:249
  295.1 18.3 %collective-permute-start.39 = (bf16[4,128,384]{2,1,0:T(8,128)(2,1)S(1)}, bf16[4,128,384]{2,1,0:T(8,128)(2,1)S(1)}, u32[]{:S(2)}, u32[]{:S(2)}) collective-permute-start(bf16[4,128,384]{2,1,0:T(8,128)(2,1)S(1)} %get-tuple-element.72), channel_id=1, source_target_pairs={{0,8},{4,12},{8,16},{12,20},{16,24},{20,28},{1,9},{5,13},{9,17},{1... | collective-permute-start | bytes 1179656 | tf_op jit(solution)/shard_map/ppermute | solution.py:334
  322.1 22.0 %collective-permute-start.37 = (bf16[2,128,384]{2,1,0:T(8,128)(2,1)S(1)}, bf16[2,128,384]{2,1,0:T(8,128)(2,1)S(1)}, u32[]{:S(2)}, u32[]{:S(2)}) collective-permute-start(bf16[2,128,384]{2,1,0:T(8,128)(2,1)S(1)} %get-tuple-element.115), channel_id=1, source_target_pairs={{0,1},{1,2},{2,3},{4,5},{5,6},{6,7},{8,9},{9,10},{10,11},{12,13},{... | collective-permute-start | bytes 589832 | tf_op jit(solution)/shard_map/ppermute | solution.py:248
  324.9 19.2 %collective-permute-start.38 = (bf16[2,128,384]{2,1,0:T(8,128)(2,1)S(1)}, bf16[2,128,384]{2,1,0:T(8,128)(2,1)S(1)}, u32[]{:S(2)}, u32[]{:S(2)}) collective-permute-start(bf16[2,128,384]{2,1,0:T(8,128)(2,1)S(1)} %get-tuple-element.114), channel_id=1, source_target_pairs={{1,0},{2,1},{3,2},{5,4},{6,5},{7,6},{9,8},{10,9},{11,10},{13,12},{... | collective-permute-start | bytes 589832 | tf_op jit(solution)/shard_map/ppermute | solution.py:249
  340.0 20.5 %collective-permute-start.47 = (bf16[4,128,384]{2,1,0:T(8,128)(2,1)}, bf16[4,128,384]{2,1,0:T(8,128)(2,1)S(1)}, u32[]{:S(2)}, u32[]{:S(2)}) collective-permute-start(bf16[4,128,384]{2,1,0:T(8,128)(2,1)} %get-tuple-element.78), channel_id=1, source_target_pairs={{0,8},{4,12},{8,16},{12,20},{16,24},{20,28},{1,9},{5,13},{9,17},{1... | collective-permute-start | bytes 1179656 | tf_op jit(solution)/shard_map/ppermute | solution.py:334
  369.2 21.5 %collective-permute-start.45 = (bf16[2,128,384]{2,1,0:T(8,128)(2,1)S(1)}, bf16[2,128,384]{2,1,0:T(8,128)(2,1)S(1)}, u32[]{:S(2)}, u32[]{:S(2)}) collective-permute-start(bf16[2,128,384]{2,1,0:T(8,128)(2,1)S(1)} %get-tuple-element.111), channel_id=1, source_target_pairs={{0,1},{1,2},{2,3},{4,5},{5,6},{6,7},{8,9},{9,10},{10,11},{12,13},{... | collective-permute-start | bytes 589832 | tf_op jit(solution)/shard_map/ppermute | solution.py:248
  372.4 18.3 %collective-permute-start.46 = (bf16[2,128,384]{2,1,0:T(8,128)(2,1)S(1)}, bf16[2,128,384]{2,1,0:T(8,128)(2,1)S(1)}, u32[]{:S(2)}, u32[]{:S(2)}) collective-permute-start(bf16[2,128,384]{2,1,0:T(8,128)(2,1)S(1)} %get-tuple-element.110), channel_id=1, source_target_pairs={{1,0},{2,1},{3,2},{5,4},{6,5},{7,6},{9,8},{10,9},{11,10},{13,12},{... | collective-permute-start | bytes 589832 | tf_op jit(solution)/shard_map/ppermute | solution.py:249
  390.7 19.3 %collective-permute-start.27 = (bf16[4,128,384]{2,1,0:T(8,128)(2,1)}, bf16[4,128,384]{2,1,0:T(8,128)(2,1)}, u32[]{:S(2)}, u32[]{:S(2)}) collective-permute-start(bf16[4,128,384]{2,1,0:T(8,128)(2,1)} %get-tuple-element.95), channel_id=1, source_target_pairs={{0,4},{4,0},{8,12},{12,8},{16,20},{20,16},{24,28},{28,24},{1,5},{5... | collective-permute-start | bytes 1179656 | tf_op jit(solution)/shard_map/ppermute | solution.py:339
  407.9 17.4 %collective-permute-start.35 = (bf16[4,128,384]{2,1,0:T(8,128)(2,1)}, bf16[4,128,384]{2,1,0:T(8,128)(2,1)}, u32[]{:S(2)}, u32[]{:S(2)}) collective-permute-start(bf16[4,128,384]{2,1,0:T(8,128)(2,1)} %get-tuple-element.94), channel_id=1, source_target_pairs={{0,4},{4,0},{8,12},{12,8},{16,20},{20,16},{24,28},{28,24},{1,5},{5... | collective-permute-start | bytes 1179656 | tf_op jit(solution)/shard_map/ppermute | solution.py:339
  408.0 32.2 %collective-permute-start.34 = (bf16[4,128,384]{2,1,0:T(8,128)(2,1)}, bf16[4,128,384]{2,1,0:T(8,128)(2,1)S(1)}, u32[]{:S(2)}, u32[]{:S(2)}) collective-permute-start(bf16[4,128,384]{2,1,0:T(8,128)(2,1)} %get-tuple-element.98), channel_id=1, source_target_pairs={{0,4},{4,0},{8,12},{12,8},{16,20},{20,16},{24,28},{28,24},{1,5},{5... | collective-permute-start | bytes 1179656 | tf_op jit(solution)/shard_map/ppermute | solution.py:339
  410.0 35.4 %collective-permute-start.43 = (bf16[4,128,384]{2,1,0:T(8,128)(2,1)}, bf16[4,128,384]{2,1,0:T(8,128)(2,1)S(1)}, u32[]{:S(2)}, u32[]{:S(2)}) collective-permute-start(bf16[4,128,384]{2,1,0:T(8,128)(2,1)} %get-tuple-element.93), channel_id=1, source_target_pairs={{0,4},{4,0},{8,12},{12,8},{16,20},{20,16},{24,28},{28,24},{1,5},{5... | collective-permute-start | bytes 1179656 | tf_op jit(solution)/shard_map/ppermute | solution.py:339
  410.0 40.6 %collective-permute-start.42 = (bf16[4,128,384]{2,1,0:T(8,128)(2,1)}, bf16[4,128,384]{2,1,0:T(8,128)(2,1)S(1)}, u32[]{:S(2)}, u32[]{:S(2)}) collective-permute-start(bf16[4,128,384]{2,1,0:T(8,128)(2,1)} %get-tuple-element.97), channel_id=1, source_target_pairs={{0,4},{4,0},{8,12},{12,8},{16,20},{20,16},{24,28},{28,24},{1,5},{5... | collective-permute-start | bytes 1179656 | tf_op jit(solution)/shard_map/ppermute | solution.py:339
  416.9 42.1 %collective-permute-start.51 = (bf16[4,128,384]{2,1,0:T(8,128)(2,1)}, bf16[4,128,384]{2,1,0:T(8,128)(2,1)S(1)}, u32[]{:S(2)}, u32[]{:S(2)}) collective-permute-start(bf16[4,128,384]{2,1,0:T(8,128)(2,1)} %get-tuple-element.92), channel_id=1, source_target_pairs={{0,4},{4,0},{8,12},{12,8},{16,20},{20,16},{24,28},{28,24},{1,5},{5... | collective-permute-start | bytes 1179656 | tf_op jit(solution)/shard_map/ppermute | solution.py:339
  425.3 42.1 %collective-permute-start.50 = (bf16[4,128,384]{2,1,0:T(8,128)(2,1)}, bf16[4,128,384]{2,1,0:T(8,128)(2,1)S(1)}, u32[]{:S(2)}, u32[]{:S(2)}) collective-permute-start(bf16[4,128,384]{2,1,0:T(8,128)(2,1)} %get-tuple-element.96), channel_id=1, source_target_pairs={{0,4},{4,0},{8,12},{12,8},{16,20},{20,16},{24,28},{28,24},{1,5},{5... | collective-permute-start | bytes 1179656 | tf_op jit(solution)/shard_map/ppermute | solution.py:339
  485.2 14.8 %collective-permute-start.53 = (bf16[1,256,1024]{2,1,0:T(8,128)(2,1)S(1)}, bf16[1,256,1024]{2,1,0:T(8,128)(2,1)S(1)}, u32[]{:S(2)}, u32[]{:S(2)}) collective-permute-start(bf16[1,256,1024]{2,1,0:T(8,128)(2,1)S(1)} %constant_dynamic-slice_fusion), channel_id=1, source_target_pairs={{0,2},{1,3},{2,0},{3,1},{4,6},{5,7},{6,4},{7,5},{8,10},{9,11},{10,... | collective-permute-start | bytes 1572872 | tf_op jit(solution)/shard_map/ppermute | solution.py:359
  (68 other events, 967.0 us)

commit v2 on v1

--- a/solution.py
+++ b/solution.py
@@ -16,6 +16,9 @@
 STACK = D * PAN
 BAND = 3 * PAN
 TERMS = D * PAIRS * D
+ROWS = 32
+SPLIT = 2
+SKEW = 2
 MIB = 1024 * 1024
 
 
@@ -51,36 +54,44 @@
     )(signs, coupling, ordering_matrix())
 
 
-def mix_rows(y_ref, mix_ref, column, res_ref):
-    lane = lax.broadcasted_iota(jnp.int32, (4, 8, 2 * KB), 2)
-    low = lane < KB
-    for chunk in range(PAN // 32):
-        start = chunk * 32
+def mix_rows(y_ref, mix_ref, column, res_ref, starts):
+    low = lax.broadcasted_iota(jnp.int32, (ROWS, 2 * KB), 1) < KB
+    for start in starts:
         acc = [None] * D
         for u in range(D):
             for q in range(PAIRS):
-                y = y_ref[u * PAN + start : u * PAN + start + 32, q * 128 : (q + 1) * 128]
-                y = y.reshape(4, 8, 128)
+                y = y_ref[u * PAN + start : u * PAN + start + ROWS, q * 128 : (q + 1) * 128]
+                y = y.reshape(ROWS // 8, 8, 128)
                 for e in range(D):
                     term = y * mix_ref[column, (u * PAIRS + q) * D + e][None]
                     acc[e] = term if acc[e] is None else acc[e] + term
         for q in range(PAIRS):
-            even, odd = acc[2 * q], acc[2 * q + 1]
-            even = even + pltpu.roll(even.reshape(32, 128), KB, 1).reshape(4, 8, 128)
-            odd = odd + pltpu.roll(odd.reshape(32, 128), KB, 1).reshape(4, 8, 128)
-            both = jnp.where(low, even, odd).reshape(32, 128)
-            res_ref[start : start + 32, q * 128 : (q + 1) * 128] = both.astype(jnp.bfloat16)
+            even, odd = acc[2 * q].reshape(ROWS, 128), acc[2 * q + 1].reshape(ROWS, 128)
+            straight = jnp.where(low, even, odd)
+            crossed = jnp.where(low, odd, even)
+            both = straight + pltpu.roll(crossed, KB, 1)
+            res_ref[start : start + ROWS, q * 128 : (q + 1) * 128] = both.astype(jnp.bfloat16)
+
+
+def dot_and_mix(y_out, band_ref, rhs, y_in, mix_ref, column, res_ref):
+    step, part = STACK // SPLIT, PAN // SPLIT
+    for i in range(SPLIT):
+        rows = slice(i * step, (i + 1) * step)
+        y_out[rows, :] = jnp.dot(band_ref[0, rows, :], rhs, preferred_element_type=jnp.float32)
+        mix_rows(y_in, mix_ref, column, res_ref, range(i * part, (i + 1) * part, ROWS))
 
 
 def turn_kernel(
     panels, odd_first, count,
-    flag_ref, left_ref, low_ref, mid_ref, high_ref, ca_ref, cb_ref, mix_ref,
+    flag_ref, left_in_ref, left_ref, left_out_ref, in_ref, mid_ref, out_ref, ca_ref, cb_ref, mix_ref,
     keep_ref, send_ref, pass_ref,
     src, ya, yb, wide, res_a, res_b,
 ):
     s = pl.program_id(0)
     is_odd_home = flag_ref[0]
     is_first = flag_ref[1]
+    inner_at = jnp.where(flag_ref[3] == 0, panels + 2, 0)
+    outer_at = panels + 2 - inner_at
     even_total = panels + 2
     dump = 2 * panels + 6
 
@@ -88,16 +99,16 @@
     def _():
         @pl.when(is_first == 1)
         def _():
-            src[0 : panels + 4] = left_ref[0]
+            src[pl.ds(inner_at, 2)] = left_in_ref[0]
+            src[2 : panels + 2] = left_ref[0]
+            src[pl.ds(outer_at, 2)] = left_out_ref[0]
 
         @pl.when(is_first == 0)
         def _():
-            src[0:2] = low_ref[...]
+            src[pl.ds(inner_at, 2)] = in_ref[...]
             src[2 : panels + 2] = mid_ref[...]
-            src[panels + 2 : panels + 4] = high_ref[...]
-
-        src[panels + 4 :] = jnp.zeros((panels + 3, PAN, LANES), jnp.bfloat16)
-        yb[...] = jnp.zeros_like(yb)
+            src[pl.ds(outer_at, 2)] = out_ref[...]
+
         for column in range(2):
             for i in range(TERMS):
                 wide[column, i] = jnp.broadcast_to(mix_ref[0, column, i : i + 1, :], (8, 128))
@@ -137,20 +148,18 @@
 
     @pl.when(s < count // 2)
     def _():
-        ya[...] = jnp.dot(ca_ref[0], window(n), preferred_element_type=jnp.float32)
-        mix_rows(yb, wide, phase(n - 1), res_b)
+        dot_and_mix(ya, ca_ref, window(n), yb, wide, phase(n - 1), res_b)
         hand_out(n - 1, res_b)
-        yb[...] = jnp.dot(cb_ref[0], window(n + 1), preferred_element_type=jnp.float32)
-        mix_rows(ya, wide, phase(n), res_a)
+        dot_and_mix(yb, cb_ref, window(n + 1), ya, wide, phase(n), res_a)
         hand_out(n, res_a)
 
     @pl.when(s == count // 2)
     def _():
-        mix_rows(yb, wide, phase(n - 1), res_b)
+        mix_rows(yb, wide, phase(n - 1), res_b, range(0, PAN, ROWS))
         hand_out(n - 1, res_b)
 
 
-def one_turn(flags, left, low, mid, high, bands, mixing):
+def one_turn(flags, left, inner, mid, outer, bands, mixing):
     panels = mid.shape[0]
     gap = 0 if panels >= 2 else 1
     odd_first = panels + 2 + gap
@@ -167,7 +176,9 @@
         num_scalar_prefetch=1,
         grid=(count // 2 + 1,),
         in_specs=[
-            pl.BlockSpec((1, panels + 4, PAN, LANES), lambda s, f: (f[2], 0, 0, 0)),
+            pl.BlockSpec((1, 2, PAN, LANES), lambda s, f: (f[2], 0, 0, 0)),
+            pl.BlockSpec((1, panels, PAN, LANES), lambda s, f: (f[2], 0, 0, 0)),
+            pl.BlockSpec((1, 2, PAN, LANES), lambda s, f: (f[2], 0, 0, 0)),
             whole((2, PAN, LANES)),
             whole((panels, PAN, LANES)),
             whole((2, PAN, LANES)),
@@ -197,45 +208,72 @@
             transcendentals=0,
         ),
         name="two_columns",
-    )(flags, left, low, mid, high, bands, bands, mixing)
-
-
-def unpack_kernel(at_ref, held_ref, one_ref, two_ref, out_ref):
-    rows = one_ref.shape[1]
-    low = lax.broadcasted_iota(jnp.int32, (rows, 128), 1) < KB
+    )(flags, *left, inner, mid, outer, bands, bands, mixing)
+
+
+def pack_kernel(at_ref, left_ref, out_ref):
+    low = lax.broadcasted_iota(jnp.int32, (PAN, 128), 1) < KB
     for q in range(PAIRS):
-        one = one_ref[0, :, q * 128 : (q + 1) * 128].astype(jnp.float32)
-        two = two_ref[0, :, q * 128 : (q + 1) * 128].astype(jnp.float32)
+        even = left_ref[2 * q].astype(jnp.float32)
+        odd = left_ref[2 * q + 1].astype(jnp.float32)
+        first = jnp.where(low, even, pltpu.roll(odd, KB, 1))
+        second = jnp.where(low, pltpu.roll(even, KB, 1), odd)
+        out_ref[0, 0, :, q * 128 : (q + 1) * 128] = first.astype(jnp.bfloat16)
+        out_ref[1, 0, :, q * 128 : (q + 1) * 128] = second.astype(jnp.bfloat16)
+
+
+def packed(at, left, blocks):
+    panels = left.shape[1] // PAN
+    return pl.pallas_call(
+        pack_kernel,
+        grid_spec=pltpu.PrefetchScalarGridSpec(
+            num_scalar_prefetch=1,
+            grid=(blocks // 2, panels),
+            in_specs=[pl.BlockSpec((D, PAN, 128), lambda c, p, f: (0, p, f[0] + c))],
+            out_specs=pl.BlockSpec((2, 1, PAN, LANES), lambda c, p, f: (c, p, 0, 0)),
+        ),
+        out_shape=jax.ShapeDtypeStruct((blocks, panels, PAN, LANES), jnp.bfloat16),
+        compiler_params=pltpu.CompilerParams(vmem_limit_bytes=32 * MIB),
+        name="pack",
+    )(at, left)
+
+
+def unpack_kernel(at_ref, ka_ref, kb_ref, ga_ref, gb_ref, *rest):
+    out_ref = rest[-1]
+    low = lax.broadcasted_iota(jnp.int32, (PAN, 128), 1) < KB
+    own = pl.program_id(0) == 0
+    for q in range(PAIRS):
+        lanes = slice(q * 128, (q + 1) * 128)
+        one = jnp.where(own, ka_ref[0, :, lanes].astype(jnp.float32), ga_ref[0, :, lanes].astype(jnp.float32))
+        two = jnp.where(own, kb_ref[0, :, lanes].astype(jnp.float32), gb_ref[0, :, lanes].astype(jnp.float32))
         first = jnp.where(low, one, pltpu.roll(two, KB, 1))
         second = jnp.where(low, pltpu.roll(one, KB, 1), two)
         out_ref[2 * q] = first.astype(jnp.bfloat16)
         out_ref[2 * q + 1] = second.astype(jnp.bfloat16)
 
 
-def unpacked(at, held, one, two):
-    panels = one.shape[0]
+def unpacked(at, held, shape, parts):
+    panels = parts[0].shape[0]
+    one = pl.BlockSpec((1, PAN, LANES), lambda s, p, f: (p, 0, 0))
+    more = [] if held is None else [held]
     return pl.pallas_call(
         unpack_kernel,
         grid_spec=pltpu.PrefetchScalarGridSpec(
             num_scalar_prefetch=1,
-            grid=(panels,),
-            in_specs=[
-                pl.BlockSpec(memory_space=pl.ANY),
-                pl.BlockSpec((1, PAN, LANES), lambda p, f: (p, 0, 0)),
-                pl.BlockSpec((1, PAN, LANES), lambda p, f: (p, 0, 0)),
-            ],
-            out_specs=pl.BlockSpec((D, PAN, 128), lambda p, f: (0, p, f[0])),
+            grid=(2, panels),
+            in_specs=[one] * 4 + [pl.BlockSpec(memory_space=pl.ANY)] * len(more),
+            out_specs=pl.BlockSpec((D, PAN, 128), lambda s, p, f: (0, p, f[s])),
         ),
-        out_shape=jax.ShapeDtypeStruct(held.shape, held.dtype),
-        input_output_aliases={1: 0},
+        out_shape=jax.ShapeDtypeStruct(shape, jnp.bfloat16),
+        input_output_aliases={5: 0} if more else {},
         compiler_params=pltpu.CompilerParams(vmem_limit_bytes=32 * MIB),
         name="unpack",
-    )(at, held, one, two)
-
-
-def edges(block, width, axis_dim=0):
+    )(at, *parts, *more)
+
+
+def far_edges(block, width, dim):
     count = lax.axis_size("sec")
-    have = block.shape[axis_dim]
+    have = block.shape[dim]
     low_parts, high_parts = [], []
     reach = 0
     while width > reach:
@@ -243,14 +281,39 @@
         take = min(have, width - reach)
         forward = [(i, i + hop) for i in range(count - hop)]
         backward = [(i + hop, i) for i in range(count - hop)]
-        top = lax.slice_in_dim(block, have - take, have, axis=axis_dim)
-        bottom = lax.slice_in_dim(block, 0, take, axis=axis_dim)
+        top = lax.slice_in_dim(block, have - take, have, axis=dim)
+        bottom = lax.slice_in_dim(block, 0, take, axis=dim)
         low_parts.insert(0, lax.ppermute(top, "sec", forward))
         high_parts.append(lax.ppermute(bottom, "sec", backward))
         reach += take
-    if len(low_parts) == 1:
-        return low_parts[0], high_parts[0]
-    return jnp.concatenate(low_parts, axis_dim), jnp.concatenate(high_parts, axis_dim)
+    low, high = jnp.concatenate(low_parts, dim), jnp.concatenate(high_parts, dim)
+    first = lax.axis_index("sec") % 2 == 0
+    return jnp.where(first, high, low), jnp.where(first, low, high)
+
+
+def side(block, width, dim, towards_inner):
+    first = lax.axis_index("sec") % 2 == 0
+    top_wanted = first if towards_inner else jnp.logical_not(first)
+    start = jnp.where(top_wanted, block.shape[dim] - width, 0)
+    return lax.dynamic_slice_in_dim(block, start, width, dim)
+
+
+def inner_edge(block, width, dim=0):
+    pairs = [(i, i ^ 1) for i in range(lax.axis_size("sec"))]
+    return lax.ppermute(side(block, width, dim, True), "sec", pairs)
+
+
+def outer_pairs():
+    count = lax.axis_size("sec")
+    forward = [(i, i + 1) for i in range(1, count - 1, 2)]
+    return forward + [(j, i) for i, j in forward]
+
+
+def both_edges(block, width, dim=0):
+    if block.shape[dim] < width:
+        return far_edges(block, width, dim)
+    outer = lax.ppermute(side(block, width, dim, False), "sec", outer_pairs())
+    return inner_edge(block, width, dim), outer
 
 
 def on_device(left_start, coupling, tensor, sketch, block_parity, leg_parity):
@@ -275,15 +338,10 @@
     table = 1.0 - 2.0 * (parity[:, None] * legs[None, :]).astype(jnp.float32)
     signs = jnp.stack([table[w : w + panels] for w in range(3)], 1).reshape(panels, 3 * D)
     own = ordered_coupling(coupling[0], signs)
-    other = lax.ppermute(own, "col", swap)
-    own_low, own_high = edges(own, 1)
-    other_low, other_high = edges(other, 1)
     odd_home = half == 1
-    even_bands = [
-        jnp.where(odd_home, b, a)
-        for a, b in ((own_low, other_low), (own, other), (own_high, other_high))
-    ]
-    bands = jnp.concatenate(even_bands + [jnp.where(odd_home, own, other)], 0)
+    rim = jnp.concatenate([own[:1], own[panels - 1 :]], 0) if panels > 1 else own
+    other_rim = lax.ppermute(rim, "col", swap)
+    own_inner, own_outer = both_edges(rim, 1)
 
     small = jnp.concatenate([tensor[0].reshape(D, D * D * D), sketch[0]], 1)
     small_other = lax.ppermute(small, "col", swap)
@@ -303,21 +361,43 @@
         1,
     )
 
-    mine = lax.dynamic_slice_in_dim(left_start, half * half_cols, half_cols, 2)
-    mine = mine.reshape(panels, PAN, PAIRS, 2, blocks, KB).transpose(4, 0, 1, 2, 3, 5)
-    mine = mine.reshape(blocks, panels, PAN, LANES)
-    left_low, left_high = edges(mine, 2, 1)
-    left = jnp.concatenate([left_low, mine, left_high], 1)
-
-    skew = 2
+    at_half = (half * (blocks // 2)).astype(jnp.int32)[None]
+    mine = packed(at_half, left_start.transpose(1, 0, 2), blocks)
+    left_inner, left_outer = both_edges(mine, 2, 1)
+
+    if panels > 2:
+        inner = own[1 : panels - 1]
+        other_inner = lax.ppermute(inner, "col", swap)
+        other = [other_rim[:1], other_inner, other_rim[1:]]
+        mine_too = [own[:1], own[1 : panels - 1], own[panels - 1 :]]
+    else:
+        other, mine_too = [other_rim], [own]
+    other_inner_edge, other_outer_edge = both_edges(other_rim, 1)
+    even_inner = jnp.where(odd_home, other_inner_edge, own_inner)
+    even_outer = jnp.where(odd_home, other_outer_edge, own_outer)
+    first_core = sec_index % 2 == 0
+    even_low = jnp.where(first_core, even_outer, even_inner)
+    even_high = jnp.where(first_core, even_inner, even_outer)
+    even_bands = [
+        jnp.where(odd_home, b, a)
+        for a, b in zip(mine_too, other)
+    ]
+    odd_bands = [jnp.where(odd_home, a, b) for a, b in zip(mine_too, other)]
+    even_bands = [even_low] + even_bands + [even_high]
+    left_inner, left_outer, mixing, *rest = lax.optimization_barrier(
+        (left_inner, left_outer, mixing, *even_bands, *odd_bands)
+    )
+    bands = jnp.concatenate(rest, 0)
+    left = (left_inner, mine, left_outer)
+
+    skew = SKEW
     turns = blocks + skew * (stages - 1)
     zero_edge = jnp.zeros((2, PAN, LANES), jnp.bfloat16)
     zero_mid = jnp.zeros((panels, PAN, LANES), jnp.bfloat16)
     arrived = {t: (zero_edge, zero_mid, zero_edge) for t in range(skew)}
     keeps, sends = {}, {}
-    kept, got = [], []
+    kept = []
     lag = skew * (stages - 1)
-    states = jnp.zeros((D, row_count, rank), jnp.bfloat16)
 
     def staged(table_of, i):
         out = table_of[i + lag]
@@ -325,43 +405,73 @@
             out = jnp.where(stage == z, table_of[i + skew * z], out)
         return out
 
+    flying, swapping = {}, {}
+    states = None
+    across = [
+        (c * sec_count + i, (c + 2) * sec_count + j)
+        for c in range(col_count - 2)
+        for i, j in outer_pairs()
+    ]
+    direct = panels >= 2
     for t in range(turns):
         index = jnp.clip(t - skew * stage, 0, blocks - 1)
-        flags = jnp.stack([half, (stage == 0).astype(jnp.int32), index]).astype(jnp.int32)
-        low, mid, high = arrived.pop(t)
-        keeps[t], sends[t], passed = one_turn(flags, left, low, mid, high, bands, mixing)
+        flags = jnp.stack([half, (stage == 0).astype(jnp.int32), index, sec_index % 2])
+        flags = flags.astype(jnp.int32)
+        inner, mid, outer = arrived.pop(t)
+        if t - 2 in swapping:
+            flags, swapping[t - 2] = lax.optimization_barrier((flags, swapping[t - 2]))
+        keeps[t], sends[t], passed = one_turn(flags, left, inner, mid, outer, bands, mixing)
+        if t - 1 in flying:
+            (nxt, outer), passed = lax.optimization_barrier((flying[t - 1], passed))
+            if direct:
+                inner = inner_edge(nxt, 2)
+            else:
+                inner, outer = far_edges(nxt, 2, 0)
+            arrived[t - 1 + skew] = (inner, nxt, outer)
         if t + skew < turns:
             nxt = lax.ppermute(passed, "col", up)
-            nlow, nhigh = edges(nxt, 2)
-            arrived[t + skew] = (nlow, nxt, nhigh)
+            edge = nxt
+            if direct:
+                edge = lax.ppermute(side(passed, 2, 0, False), ("col", "sec"), across)
+            flying[t] = (nxt, edge)
         if t >= lag:
             i = t - lag
-            got.append(lax.ppermute(staged(sends, i), "col", swap))
+            swapping[t] = lax.ppermute(staged(sends, i), "col", swap)
             kept.append(staged(keeps, i))
-            if i % 2 == 1:
-                at_own = (half * (blocks // 2) + i // 2).astype(jnp.int32)[None]
-                at_got = ((1 - half) * (blocks // 2) + i // 2).astype(jnp.int32)[None]
-                states = unpacked(at_own, states, kept[i - 1], kept[i])
-                states = unpacked(at_got, states, got[i - 1], got[i])
+        for j in range(1, blocks, 2):
+            if t == j + lag + 2 or (t == turns - 1 and j + lag + 2 > t):
+                at = jnp.stack([half, 1 - half]) * (blocks // 2) + j // 2
+                parts = (kept[j - 1], kept[j], swapping[j - 1 + lag], swapping[j + lag])
+                states = unpacked(at.astype(jnp.int32), states, (D, row_count, rank), parts)
 
     flat = states.reshape(D * row_count, rank)
-    partial = lax.dot_general(
-        flat, flat, (((0,), (0,)), ((), ())), preferred_element_type=jnp.float32
-    ).astype(jnp.bfloat16)
     share = rank // sec_count
-    gram = partial.reshape(sec_count, share, rank)
-    width = 1
-    while width < sec_count:
-        bit = (sec_index // width) % 2
-        pairs = gram.reshape(-1, 2, share, rank)
-        stay = lax.dynamic_index_in_dim(pairs, bit, 1, keepdims=False)
-        away = lax.dynamic_index_in_dim(pairs, 1 - bit, 1, keepdims=False)
-        come = lax.ppermute(away, "sec", [(i, i ^ width) for i in range(sec_count)])
-        gram = stay.astype(jnp.float32) + come.astype(jnp.float32)
-        if gram.shape[0] > 1:
-            gram = gram.astype(jnp.bfloat16)
-        width *= 2
-    gram_out = gram * (1.0 / (CHI * D))
+    group = sec_count // 2
+    top = sec_index // group
+    halves = {}
+    for name, which in (("far", 1 - top), ("near", top)):
+        columns = lax.dynamic_slice_in_dim(flat, which * (rank // 2), rank // 2, 1)
+        if name == "near":
+            columns, far_now = lax.optimization_barrier((columns, halves["far"]))
+            halves["far"] = far_now
+            crossed = lax.ppermute(far_now, "sec", [(i, i ^ group) for i in range(sec_count)])
+        gram = lax.dot_general(
+            columns, flat, (((0,), (0,)), ((), ())), preferred_element_type=jnp.float32
+        ).astype(jnp.bfloat16)
+        gram = gram.reshape(group, share, rank)
+        width = 1
+        while width < group:
+            bit = (sec_index // width) % 2
+            pairs = gram.reshape(-1, 2, share, rank)
+            stay = lax.dynamic_index_in_dim(pairs, bit, 1, keepdims=False)
+            away = lax.dynamic_index_in_dim(pairs, 1 - bit, 1, keepdims=False)
+            come = lax.ppermute(away, "sec", [(i, i ^ width) for i in range(sec_count)])
+            gram = stay.astype(jnp.float32) + come.astype(jnp.float32)
+            if name == "far" or gram.shape[0] > 1:
+                gram = gram.astype(jnp.bfloat16)
+            width *= 2
+        halves[name] = gram
+    gram_out = (halves["near"].astype(jnp.float32) + crossed.astype(jnp.float32)) * (1.0 / (CHI * D))
     return states.transpose(1, 0, 2)[None], gram_out
 
 

time: 511 us -> 421 us (0.82)
  starting transfers between devices: 134 us -> 78 us
  waiting for transfers between devices: 81.3 us -> 42.2 us
  local copies, waits for them, and re-layouts: 54.2 us -> 59.8 us
    ppermute x39 -> x41, starting transfers between devices: 90.7 us -> 51.8 us  [the longest x15 26.8 us: inner_edge(): return lax.ppermute(side(block, width, dim, True), 'sec', pairs)]
    ppermute x12, waiting for transfers between devices: 23.2 us -> 0.03 us  [on_device(): nxt = lax.ppermute(passed, 'col', up)]
    unnamed x94 -> x152, local copies, waits for them, and re-layouts: 13.8 us -> 36.6 us
    ppermute x12, starting transfers between devices: 39 us -> 22.7 us  [on_device(): nxt = lax.ppermute(passed, 'col', up)]
    ppermute x1, waiting for transfers between devices: 13.9 us -> 0.01 us  [on_device(): small_other = lax.ppermute(small, 'col', swap)]
    ppermute x2, waiting for transfers between devices: 14.6 us -> 1.06 us  [on_device(): come = lax.ppermute(away, 'sec', [(i, i ^ width) for i in range(sec_count)])]
    ppermute x39 -> x41, waiting for transfers between devices: 29.6 us -> 41.2 us  [the longest x1 17.4 us: on_device(): other_inner = lax.ppermute(inner, 'col', swap)]
    reshape x2 -> x0, local copies, waits for them, and re-layouts: 10.1 us -> none  [the longest x1 5.49 us: on_device(): mine.reshape(panels, PAN, PAIRS, 2, blocks, KB).transpose(4, 0, 1, 2, 3, 5)]
  transfers between devices with their start and end apart: 54 -> 56, of which waited for: 14 -> 5; matrix products, arithmetic and copies ran while one was open for 11% -> 10% of each run, Pallas kernels for 35% -> 44%
where the time goes in v2:
time: 421 us; the launch traced here: 414 us
  Pallas kernels  197 us (47%)
  starting transfers between devices  78 us (19%)
  local copies, waits for them, and re-layouts  59.8 us (14%)
  waiting for transfers between devices  42.2 us (10%)
  other arithmetic  20.6 us (5%)
  matrix products  13.8 us (3%)
    pallas_call x14, Pallas kernels, one_turn(): pl.pallas_call(functools.partial(turn_kernel, panels, odd_first, count),...  173 us
    unnamed x152, local copies, waits for them, and re-layouts  36.6 us
    ppermute x15, starting transfers between devices, inner_edge(): return lax.ppermute(side(block, width, dim, True), 'sec', pairs)  26.8 us
    ppermute x12, starting transfers between devices, on_device(): nxt = lax.ppermute(passed, 'col', up)  22.7 us
    ppermute x1, waiting for transfers between devices, on_device(): other_inner = lax.ppermute(inner, 'col', swap)  17.4 us
    pallas_call x4, Pallas kernels, unpacked(): pl.pallas_call(unpack_kernel, grid_spec=pltpu.PrefetchScalarGridSpec(num_...  16 us
    ppermute x1, waiting for transfers between devices, on_device(): lax.ppermute(far_now, 'sec', [(i, i ^ group) for i in range(sec_count)])  12.4 us
    ppermute x1, waiting for transfers between devices, on_device(): other_rim = lax.ppermute(rim, 'col', swap)  11.1 us
  transfers between devices with their start and end apart: 56, of which 5 were waited for; matrix products, arithmetic and copies ran while one was open for 10% of the time, Pallas kernels for 44%

profile of v2, /device:TPU:0, one launch (start us, length us, event | category | flops | bytes accessed | tf_op | source)
XLA Modules:
  0.0 414.3 jit_solution(10316470536704941364)
XLA Ops:
  2.8 2.9 collective-permute-start.2
  9.5 5.3 %order_coupling.1 = bf16[4,768,384]{2,1,0:T(8,128)(2,1)S(1)} custom-call(f32[4,18]{1,0:T(4,128)S(1)} %reshape.49.sign_ref, bf16[512,2304]{1,0:T(8,128)(2,1)S(1)} %bitcast.72, bf16[768,768]{1,0:T(8,128)(2,1)S(1)} %fusion.2.perm_ref), custom_call_target="tpu_custom_call" | custom-call | tf_op jit(solution)/shard_map/order_coupling/pallas_call | solution.py:42
  20.9 2.8 copy-done.8
  23.7 3.4 pack.1.left_ref
  35.8 11.1 %collective-permute-done.3 = bf16[2,768,384]{2,1,0:T(8,128)(2,1)} collective-permute-done((bf16[2,768,384]{2,1,0:T(8,128)(2,1)}, bf16[2,768,384]{2,1,0:T(8,128)(2,1)}, u32[]{:S(2)}, u32[]{:S(2)}) %collective-permute-start.3) | collective-permute-done | bytes 1179680 | tf_op jit(solution)/shard_map/ppermute | solution.py:343
  48.3 3.9 broadcast_select_fusion.2
  54.3 17.4 %collective-permute-done.8 = bf16[2,768,384]{2,1,0:T(8,128)(2,1)} collective-permute-done((bf16[2,768,384]{2,1,0:T(8,128)(2,1)}, bf16[2,768,384]{2,1,0:T(8,128)(2,1)}, u32[]{:S(2)}, u32[]{:S(2)}) %collective-permute-start.8) | collective-permute-done | bytes 1179680 | tf_op jit(solution)/shard_map/ppermute | solution.py:370
  79.5 2.9 copy.30
  94.7 12.2 %two_columns.14 = (bf16[4,128,384]{2,1,0:T(8,128)(2,1)S(1)}, bf16[4,128,384]{2,1,0:T(8,128)(2,1)S(1)}, bf16[4,128,384]{2,1,0:T(8,128)(2,1)S(1)}) custom-call(s32[4]{0:T(128)S(1)} %get-tuple-element.247.flag_ref, bf16[8,2,128,384]{3,2,1,0:T(8,128)(2,1)} %collective-permute-done.left_in_ref, bf16[8,4,128,384]{3,2,1,0:T(8,128)(2,1)S(1)} %pack.1.left_ref, ...), custom_call_target="tpu_custom_call" | custom-call | flops 4529848320 | bytes 17694720 | tf_op jit(solution)/shard_map/two_columns/pallas_call | solution.py:200
  107.7 3.5 collective-permute-start.9
  111.9 12.2 %two_columns.15 = (bf16[4,128,384]{2,1,0:T(8,128)(2,1)S(1)}, bf16[4,128,384]{2,1,0:T(8,128)(2,1)S(1)}, bf16[4,128,384]{2,1,0:T(8,128)(2,1)S(1)}) custom-call(s32[4]{0:T(128)S(1)} %get-tuple-element.246.flag_ref, bf16[8,2,128,384]{3,2,1,0:T(8,128)(2,1)} %collective-permute-done.left_in_ref, bf16[8,4,128,384]{3,2,1,0:T(8,128)(2,1)S(1)} %pack.1.left_ref, ...), custom_call_target="tpu_custom_call" | custom-call | flops 4529848320 | bytes 17694720 | tf_op jit(solution)/shard_map/two_columns/pallas_call | solution.py:200
  127.8 4.3 %collective-permute-start.13 = (bf16[2,128,384]{2,1,0:T(8,128)(2,1)}, bf16[2,128,384]{2,1,0:T(8,128)(2,1)}, u32[]{:S(2)}, u32[]{:S(2)}) collective-permute-start(bf16[2,128,384]{2,1,0:T(8,128)(2,1)} %constant_dynamic-slice_fusion.22), channel_id=1, source_target_pairs={{0,1},{1,0},{2,3},{3,2},{4,5},{5,4},{6,7},{7,6},{8,9},{9,8},{10,11... | collective-permute-start | bytes 589832 | tf_op jit(solution)/shard_map/ppermute | solution.py:303
  132.8 3.5 collective-permute-start.11
  140.3 12.3 %two_columns.16 = (bf16[4,128,384]{2,1,0:T(8,128)(2,1)S(1)}, bf16[4,128,384]{2,1,0:T(8,128)(2,1)S(1)}, bf16[4,128,384]{2,1,0:T(8,128)(2,1)S(1)}) custom-call(s32[4]{0:T(128)S(1)} %get-tuple-element.245.flag_ref, bf16[8,2,128,384]{3,2,1,0:T(8,128)(2,1)} %collective-permute-done.left_in_ref, bf16[8,4,128,384]{3,2,1,0:T(8,128)(2,1)S(1)} %pack.1.left_ref, ...), custom_call_target="tpu_custom_call" | custom-call | flops 4529848320 | bytes 17694720 | tf_op jit(solution)/shard_map/two_columns/pallas_call | solution.py:200
  165.4 12.2 %two_columns.17 = (bf16[4,128,384]{2,1,0:T(8,128)(2,1)S(1)}, bf16[4,128,384]{2,1,0:T(8,128)(2,1)S(1)}, bf16[4,128,384]{2,1,0:T(8,128)(2,1)S(1)}) custom-call(s32[4]{0:T(128)S(1)} %copy-done.54, bf16[8,2,128,384]{3,2,1,0:T(8,128)(2,1)} %collective-permute-done.left_in_ref, bf16[8,4,128,384]{3,2,1,0:T(8,128)(2,1)S(1)} %pack.1.left_ref, ...), custom_call_target="tpu_custom_call" | custom-call | flops 4529848320 | bytes 17694720 | tf_op jit(solution)/shard_map/two_columns/pallas_call | solution.py:200
  182.4 12.2 %two_columns.18 = (bf16[4,128,384]{2,1,0:T(8,128)(2,1)S(1)}, bf16[4,128,384]{2,1,0:T(8,128)(2,1)S(1)}, bf16[4,128,384]{2,1,0:T(8,128)(2,1)S(1)}) custom-call(s32[4]{0:T(128)S(1)} %copy-done.53, bf16[8,2,128,384]{3,2,1,0:T(8,128)(2,1)} %collective-permute-done.left_in_ref, bf16[8,4,128,384]{3,2,1,0:T(8,128)(2,1)S(1)} %pack.1.left_ref, ...), custom_call_target="tpu_custom_call" | custom-call | flops 4529848320 | bytes 17694720 | tf_op jit(solution)/shard_map/two_columns/pallas_call | solution.py:200
  207.1 12.3 %two_columns.19 = (bf16[4,128,384]{2,1,0:T(8,128)(2,1)S(1)}, bf16[4,128,384]{2,1,0:T(8,128)(2,1)S(1)}, bf16[4,128,384]{2,1,0:T(8,128)(2,1)S(1)}) custom-call(s32[4]{0:T(128)S(1)} %copy-done.52, bf16[8,2,128,384]{3,2,1,0:T(8,128)(2,1)} %collective-permute-done.left_in_ref, bf16[8,4,128,384]{3,2,1,0:T(8,128)(2,1)S(1)} %pack.1.left_ref, ...), custom_call_target="tpu_custom_call" | custom-call | flops 4529848320 | bytes 17694720 | tf_op jit(solution)/shard_map/two_columns/pallas_call | solution.py:200
  231.7 12.3 %two_columns.20 = (bf16[4,128,384]{2,1,0:T(8,128)(2,1)S(1)}, bf16[4,128,384]{2,1,0:T(8,128)(2,1)S(1)}, bf16[4,128,384]{2,1,0:T(8,128)(2,1)S(1)}) custom-call(s32[4]{0:T(128)S(1)} %get-tuple-element.248.flag_ref, bf16[8,2,128,384]{3,2,1,0:T(8,128)(2,1)} %collective-permute-done.left_in_ref, bf16[8,4,128,384]{3,2,1,0:T(8,128)(2,1)S(1)} %pack.1.left_ref, ...), custom_call_target="tpu_custom_call" | custom-call | flops 4529848320 | bytes 17694720 | tf_op jit(solution)/shard_map/two_columns/pallas_call | solution.py:200
  248.9 12.2 %two_columns.21 = (bf16[4,128,384]{2,1,0:T(8,128)(2,1)S(1)}, bf16[4,128,384]{2,1,0:T(8,128)(2,1)S(1)}, bf16[4,128,384]{2,1,0:T(8,128)(2,1)S(1)}) custom-call(s32[4]{0:T(128)S(1)} %copy-done.51, bf16[8,2,128,384]{3,2,1,0:T(8,128)(2,1)} %collective-permute-done.left_in_ref, bf16[8,4,128,384]{3,2,1,0:T(8,128)(2,1)S(1)} %pack.1.left_ref, ...), custom_call_target="tpu_custom_call" | custom-call | flops 4529848320 | bytes 17694720 | tf_op jit(solution)/shard_map/two_columns/pallas_call | solution.py:200
  266.8 12.2 %two_columns.22 = (bf16[4,128,384]{2,1,0:T(8,128)(2,1)S(1)}, bf16[4,128,384]{2,1,0:T(8,128)(2,1)S(1)}, bf16[4,128,384]{2,1,0:T(8,128)(2,1)S(1)}) custom-call(s32[4]{0:T(128)S(1)} %get-tuple-element.137.flag_ref, bf16[8,2,128,384]{3,2,1,0:T(8,128)(2,1)} %collective-permute-done.left_in_ref, bf16[8,4,128,384]{3,2,1,0:T(8,128)(2,1)S(1)} %pack.1.left_ref, ...), custom_call_target="tpu_custom_call" | custom-call | flops 4529848320 | bytes 17694720 | tf_op jit(solution)/shard_map/two_columns/pallas_call | solution.py:200
  284.0 12.2 %two_columns.23 = (bf16[4,128,384]{2,1,0:T(8,128)(2,1)S(1)}, bf16[4,128,384]{2,1,0:T(8,128)(2,1)S(1)}, bf16[4,128,384]{2,1,0:T(8,128)(2,1)S(1)}) custom-call(s32[4]{0:T(128)S(1)} %copy-done.50, bf16[8,2,128,384]{3,2,1,0:T(8,128)(2,1)} %collective-permute-done.left_in_ref, bf16[8,4,128,384]{3,2,1,0:T(8,128)(2,1)S(1)} %pack.1.left_ref, ...), custom_call_target="tpu_custom_call" | custom-call | flops 4529848320 | bytes 17694720 | tf_op jit(solution)/shard_map/two_columns/pallas_call | solution.py:200
  301.8 12.2 %two_columns.24 = (bf16[4,128,384]{2,1,0:T(8,128)(2,1)S(1)}, bf16[4,128,384]{2,1,0:T(8,128)(2,1)S(1)}, bf16[4,128,384]{2,1,0:T(8,128)(2,1)S(1)}) custom-call(s32[4]{0:T(128)S(1)} %copy-done.59, bf16[8,2,128,384]{3,2,1,0:T(8,128)(2,1)} %collective-permute-done.left_in_ref, bf16[8,4,128,384]{3,2,1,0:T(8,128)(2,1)S(1)} %pack.1.left_ref, ...), custom_call_target="tpu_custom_call" | custom-call | flops 4529848320 | bytes 17694720 | tf_op jit(solution)/shard_map/two_columns/pallas_call | solution.py:200
  319.1 12.2 %two_columns.25 = (bf16[4,128,384]{2,1,0:T(8,128)(2,1)S(1)}, bf16[4,128,384]{2,1,0:T(8,128)(2,1)S(1)}, bf16[4,128,384]{2,1,0:T(8,128)(2,1)S(1)}) custom-call(s32[4]{0:T(128)S(1)} %get-tuple-element.170.flag_ref, bf16[8,2,128,384]{3,2,1,0:T(8,128)(2,1)} %collective-permute-done.left_in_ref, bf16[8,4,128,384]{3,2,1,0:T(8,128)(2,1)S(1)} %pack.1.left_ref, ...), custom_call_target="tpu_custom_call" | custom-call | flops 4529848320 | bytes 17694720 | tf_op jit(solution)/shard_map/two_columns/pallas_call | solution.py:200
  336.9 12.9 %two_columns.26 = (bf16[4,128,384]{2,1,0:T(8,128)(2,1)S(1)}, bf16[4,128,384]{2,1,0:T(8,128)(2,1)S(1)}, bf16[4,128,384]{2,1,0:T(8,128)(2,1)}) custom-call(s32[4]{0:T(128)S(1)} %get-tuple-element.165.flag_ref, bf16[8,2,128,384]{3,2,1,0:T(8,128)(2,1)} %collective-permute-done.left_in_ref, bf16[8,4,128,384]{3,2,1,0:T(8,128)(2,1)S(1)} %pack.1.left_ref, ...), custom_call_target="tpu_custom_call" | custom-call | flops 4529848320 | bytes 17694720 | tf_op jit(solution)/shard_map/two_columns/pallas_call | solution.py:200
  352.7 12.9 %two_columns.27 = (bf16[4,128,384]{2,1,0:T(8,128)(2,1)S(1)}, bf16[4,128,384]{2,1,0:T(8,128)(2,1)S(1)}, bf16[4,128,384]{2,1,0:T(8,128)(2,1)}) custom-call(s32[4]{0:T(128)S(1)} %copy-done.55, bf16[8,2,128,384]{3,2,1,0:T(8,128)(2,1)} %collective-permute-done.left_in_ref, bf16[8,4,128,384]{3,2,1,0:T(8,128)(2,1)S(1)} %pack.1.left_ref, ...), custom_call_target="tpu_custom_call" | custom-call | flops 4529848320 | bytes 17694720 | tf_op jit(solution)/shard_map/two_columns/pallas_call | solution.py:200
  367.8 3.9 unpack.4.rest_0_
  371.8 3.9 unpack.5.rest_0_
  375.7 3.9 unpack.6.rest_0_
  379.6 4.2 %unpack.7 = bf16[6,512,1024]{2,1,0:T(8,128)(2,1)} custom-call(s32[2]{0:T(128)S(1)} %copy-done.60, bf16[4,128,384]{2,1,0:T(8,128)(2,1)S(1)} %get-tuple-element.225.ka_ref, bf16[4,128,384]{2,1,0:T(8,128)(2,1)S(1)} %get-tuple-element.221.kb_ref, bf16[4,128,384]{2,1,0:T(8,128)(2,1)S(1)} %collective-permute-done.51.ga_ref, ...), custom_call_target="tpu_custom_call", output_to_operand_aliasing={{}: (5, {})} | custom-call | tf_op jit(solution)/shard_map/unpack/pallas_call | solution.py:259
  383.8 7.2 %fusion.3 = bf16[512,1024]{1,0:T(8,128)(2,1)S(1)} fusion(bf16[3072,1024]{1,0:T(8,128)(2,1)} %bitcast.73, s32[]{:T(128)S(6)} %select_n.561), kind=kOutput, calls=%fused_computation.4 | convolution fusion | flops 3221749760 | bytes 10485764 | tf_op jit(solution)/shard_map/dot_general | solution.py:458
  394.9 3.4 convolution_convert_fusion
  400.4 12.4 %collective-permute-done.55 = bf16[1,256,1024]{2,1,0:T(8,128)(2,1)S(1)} collective-permute-done((bf16[1,256,1024]{2,1,0:T(8,128)(2,1)S(1)}, bf16[1,256,1024]{2,1,0:T(8,128)(2,1)S(1)}, u32[]{:S(2)}, u32[]{:S(2)}) %collective-permute-start.55) | collective-permute-done | bytes 524320 | tf_op jit(solution)/shard_map/ppermute | solution.py:457
  (340 shorter events, 139.2 us)
Async XLA Ops:
  2.8 29.1 %collective-permute-start.2 = (f32[6,1240]{1,0:T(8,128)S(1)}, f32[6,1240]{1,0:T(8,128)S(1)}, u32[]{:S(2)}, u32[]{:S(2)}) collective-permute-start(f32[6,1240]{1,0:T(8,128)S(1)} %pad_maximum_fusion.2), channel_id=1, source_target_pairs={{0,4},{4,0},{8,12},{12,8},{16,20},{20,16},{24,28},{28,24},{1,5},{5... | collective-permute-start | bytes 89288 | tf_op jit(solution)/shard_map/ppermute | solution.py:347
  16.5 35.7 %collective-permute-start.7 = (bf16[1,768,384]{2,1,0:T(8,128)(2,1)}, bf16[1,768,384]{2,1,0:T(8,128)(2,1)}, u32[]{:S(2)}, u32[]{:S(2)}) collective-permute-start(bf16[1,768,384]{2,1,0:T(8,128)(2,1)} %get-tuple-element.228), channel_id=1, source_target_pairs={{0,1},{1,0},{2,3},{3,2},{4,5},{5,4},{6,7},{7,6},{8,9},{9,8},{10,11... | collective-permute-start | bytes 1769480 | tf_op jit(solution)/shard_map/ppermute | solution.py:303
  17.8 29.1 %collective-permute-start.3 = (bf16[2,768,384]{2,1,0:T(8,128)(2,1)}, bf16[2,768,384]{2,1,0:T(8,128)(2,1)}, u32[]{:S(2)}, u32[]{:S(2)}) collective-permute-start(bf16[2,768,384]{2,1,0:T(8,128)(2,1)} %pad_maximum_fusion), channel_id=1, source_target_pairs={{0,4},{4,0},{8,12},{12,8},{16,20},{20,16},{24,28},{28,24},{1,5},{5... | collective-permute-start | bytes 3538952 | tf_op jit(solution)/shard_map/ppermute | solution.py:343
  18.9 52.8 %collective-permute-start.8 = (bf16[2,768,384]{2,1,0:T(8,128)(2,1)}, bf16[2,768,384]{2,1,0:T(8,128)(2,1)}, u32[]{:S(2)}, u32[]{:S(2)}) collective-permute-start(bf16[2,768,384]{2,1,0:T(8,128)(2,1)} %slice.48), channel_id=1, source_target_pairs={{0,4},{4,0},{8,12},{12,8},{16,20},{20,16},{24,28},{28,24},{1,5},{5... | collective-permute-start | bytes 3538952 | tf_op jit(solution)/shard_map/ppermute | solution.py:370
  29.3 60.4 %collective-permute-start.1 = (bf16[8,2,128,384]{3,2,1,0:T(8,128)(2,1)}, bf16[8,2,128,384]{3,2,1,0:T(8,128)(2,1)}, u32[]{:S(2)}, u32[]{:S(2)}) collective-permute-start(bf16[8,2,128,384]{3,2,1,0:T(8,128)(2,1)} %get-tuple-element.212), channel_id=1, source_target_pairs={{1,2},{2,1},{5,6},{6,5},{9,10},{10,9},{13,14},{14,13},{17,18},{18,... | collective-permute-start | bytes 4718600 | tf_op jit(solution)/shard_map/ppermute | solution.py:315
  32.3 57.4 %collective-permute-start = (bf16[8,2,128,384]{3,2,1,0:T(8,128)(2,1)}, bf16[8,2,128,384]{3,2,1,0:T(8,128)(2,1)}, u32[]{:S(2)}, u32[]{:S(2)}) collective-permute-start(bf16[8,2,128,384]{3,2,1,0:T(8,128)(2,1)} %get-tuple-element.213), channel_id=1, source_target_pairs={{0,1},{1,0},{2,3},{3,2},{4,5},{5,4},{6,7},{7,6},{8,9},{9,8},{10,11... | collective-permute-start | bytes 4718600 | tf_op jit(solution)/shard_map/ppermute | solution.py:303
  46.8 41.4 %collective-permute-start.5 = (bf16[1,768,384]{2,1,0:T(8,128)(2,1)}, bf16[1,768,384]{2,1,0:T(8,128)(2,1)}, u32[]{:S(2)}, u32[]{:S(2)}) collective-permute-start(bf16[1,768,384]{2,1,0:T(8,128)(2,1)} %get-tuple-element.229), channel_id=1, source_target_pairs={{1,2},{2,1},{5,6},{6,5},{9,10},{10,9},{13,14},{14,13},{17,18},{18,... | collective-permute-start | bytes 1769480 | tf_op jit(solution)/shard_map/ppermute | solution.py:315
  52.3 36.0 %collective-permute-start.6 = (bf16[1,768,384]{2,1,0:T(8,128)(2,1)}, bf16[1,768,384]{2,1,0:T(8,128)(2,1)}, u32[]{:S(2)}, u32[]{:S(2)}) collective-permute-start(bf16[1,768,384]{2,1,0:T(8,128)(2,1)} %get-tuple-element.226), channel_id=1, source_target_pairs={{0,1},{1,0},{2,3},{3,2},{4,5},{5,4},{6,7},{7,6},{8,9},{9,8},{10,11... | collective-permute-start | bytes 1769480 | tf_op jit(solution)/shard_map/ppermute | solution.py:303
  71.7 16.5 %collective-permute-start.4 = (bf16[1,768,384]{2,1,0:T(8,128)(2,1)}, bf16[1,768,384]{2,1,0:T(8,128)(2,1)}, u32[]{:S(2)}, u32[]{:S(2)}) collective-permute-start(bf16[1,768,384]{2,1,0:T(8,128)(2,1)} %get-tuple-element.227), channel_id=1, source_target_pairs={{1,2},{2,1},{5,6},{6,5},{9,10},{10,9},{13,14},{14,13},{17,18},{18,... | collective-permute-start | bytes 1769480 | tf_op jit(solution)/shard_map/ppermute | solution.py:315
  107.7 19.5 %collective-permute-start.9 = (bf16[4,128,384]{2,1,0:T(8,128)(2,1)S(1)}, bf16[4,128,384]{2,1,0:T(8,128)(2,1)S(1)}, u32[]{:S(2)}, u32[]{:S(2)}) collective-permute-start(bf16[4,128,384]{2,1,0:T(8,128)(2,1)S(1)} %get-tuple-element.113), channel_id=1, source_target_pairs={{0,8},{4,12},{8,16},{12,20},{16,24},{20,28},{1,9},{5,13},{9,17},{1... | collective-permute-start | bytes 1179656 | tf_op jit(solution)/shard_map/ppermute | solution.py:432
  111.2 15.3 %collective-permute-start.10 = (bf16[2,128,384]{2,1,0:T(8,128)(2,1)S(1)}, bf16[2,128,384]{2,1,0:T(8,128)(2,1)S(1)}, u32[]{:S(2)}, u32[]{:S(2)}) collective-permute-start(bf16[2,128,384]{2,1,0:T(8,128)(2,1)S(1)} %constant_dynamic-slice_fusion.24), channel_id=1, source_target_pairs={{1,10},{2,9},{5,14},{6,13},{9,18},{10,17},{13,22},{14,21},{17,26},... | collective-permute-start | bytes 589832 | tf_op jit(solution)/shard_map/ppermute | solution.py:435
  132.8 22.0 %collective-permute-start.11 = (bf16[4,128,384]{2,1,0:T(8,128)(2,1)}, bf16[4,128,384]{2,1,0:T(8,128)(2,1)S(1)}, u32[]{:S(2)}, u32[]{:S(2)}) collective-permute-start(bf16[4,128,384]{2,1,0:T(8,128)(2,1)} %copy-done.47), channel_id=1, source_target_pairs={{0,8},{4,12},{8,16},{12,20},{16,24},{20,28},{1,9},{5,13},{9,17},{1... | collective-permute-start | bytes 1179656 | tf_op jit(solution)/shard_map/ppermute | solution.py:432
  137.3 16.9 %collective-permute-start.12 = (bf16[2,128,384]{2,1,0:T(8,128)(2,1)S(1)}, bf16[2,128,384]{2,1,0:T(8,128)(2,1)S(1)}, u32[]{:S(2)}, u32[]{:S(2)}) collective-permute-start(bf16[2,128,384]{2,1,0:T(8,128)(2,1)S(1)} %constant_dynamic-slice_fusion.23), channel_id=1, source_target_pairs={{1,10},{2,9},{5,14},{6,13},{9,18},{10,17},{13,22},{14,21},{17,26},... | collective-permute-start | bytes 589832 | tf_op jit(solution)/shard_map/ppermute | solution.py:435
  158.5 19.2 %collective-permute-start.14 = (bf16[4,128,384]{2,1,0:T(8,128)(2,1)}, bf16[4,128,384]{2,1,0:T(8,128)(2,1)S(1)}, u32[]{:S(2)}, u32[]{:S(2)}) collective-permute-start(bf16[4,128,384]{2,1,0:T(8,128)(2,1)} %copy-done.49), channel_id=1, source_target_pairs={{0,8},{4,12},{8,16},{12,20},{16,24},{20,28},{1,9},{5,13},{9,17},{1... | collective-permute-start | bytes 1179656 | tf_op jit(solution)/shard_map/ppermute | solution.py:432
  161.0 16.6 %collective-permute-start.15 = (bf16[2,128,384]{2,1,0:T(8,128)(2,1)S(1)}, bf16[2,128,384]{2,1,0:T(8,128)(2,1)S(1)}, u32[]{:S(2)}, u32[]{:S(2)}) collective-permute-start(bf16[2,128,384]{2,1,0:T(8,128)(2,1)S(1)} %constant_dynamic-slice_fusion.21), channel_id=1, source_target_pairs={{1,10},{2,9},{5,14},{6,13},{9,18},{10,17},{13,22},{14,21},{17,26},... | collective-permute-start | bytes 589832 | tf_op jit(solution)/shard_map/ppermute | solution.py:435
  180.0 16.0 %collective-permute-start.17 = (bf16[4,128,384]{2,1,0:T(8,128)(2,1)S(1)}, bf16[4,128,384]{2,1,0:T(8,128)(2,1)S(1)}, u32[]{:S(2)}, u32[]{:S(2)}) collective-permute-start(bf16[4,128,384]{2,1,0:T(8,128)(2,1)S(1)} %get-tuple-element.123), channel_id=1, source_target_pairs={{0,8},{4,12},{8,16},{12,20},{16,24},{20,28},{1,9},{5,13},{9,17},{1... | collective-permute-start | bytes 1179656 | tf_op jit(solution)/shard_map/ppermute | solution.py:432
  199.8 21.9 %collective-permute-start.20 = (bf16[4,128,384]{2,1,0:T(8,128)(2,1)}, bf16[4,128,384]{2,1,0:T(8,128)(2,1)S(1)}, u32[]{:S(2)}, u32[]{:S(2)}) collective-permute-start(bf16[4,128,384]{2,1,0:T(8,128)(2,1)} %copy-done.48), channel_id=1, source_target_pairs={{0,8},{4,12},{8,16},{12,20},{16,24},{20,28},{1,9},{5,13},{9,17},{1... | collective-permute-start | bytes 1179656 | tf_op jit(solution)/shard_map/ppermute | solution.py:432
  202.3 18.6 %collective-permute-start.21 = (bf16[2,128,384]{2,1,0:T(8,128)(2,1)S(1)}, bf16[2,128,384]{2,1,0:T(8,128)(2,1)S(1)}, u32[]{:S(2)}, u32[]{:S(2)}) collective-permute-start(bf16[2,128,384]{2,1,0:T(8,128)(2,1)S(1)} %constant_dynamic-slice_fusion.17), channel_id=1, source_target_pairs={{1,10},{2,9},{5,14},{6,13},{9,18},{10,17},{13,22},{14,21},{17,26},... | collective-permute-start | bytes 589832 | tf_op jit(solution)/shard_map/ppermute | solution.py:435
  225.3 18.7 %collective-permute-start.25 = (bf16[4,128,384]{2,1,0:T(8,128)(2,1)}, bf16[4,128,384]{2,1,0:T(8,128)(2,1)S(1)}, u32[]{:S(2)}, u32[]{:S(2)}) collective-permute-start(bf16[4,128,384]{2,1,0:T(8,128)(2,1)} %copy-done.46), channel_id=1, source_target_pairs={{0,8},{4,12},{8,16},{12,20},{16,24},{20,28},{1,9},{5,13},{9,17},{1... | collective-permute-start | bytes 1179656 | tf_op jit(solution)/shard_map/ppermute | solution.py:432
  227.9 16.1 %collective-permute-start.26 = (bf16[2,128,384]{2,1,0:T(8,128)(2,1)S(1)}, bf16[2,128,384]{2,1,0:T(8,128)(2,1)S(1)}, u32[]{:S(2)}, u32[]{:S(2)}) collective-permute-start(bf16[2,128,384]{2,1,0:T(8,128)(2,1)S(1)} %constant_dynamic-slice_fusion.14), channel_id=1, source_target_pairs={{1,10},{2,9},{5,14},{6,13},{9,18},{10,17},{13,22},{14,21},{17,26},... | collective-permute-start | bytes 589832 | tf_op jit(solution)/shard_map/ppermute | solution.py:435
  245.8 17.2 %collective-permute-start.24 = (bf16[4,128,384]{2,1,0:T(8,128)(2,1)S(1)}, bf16[4,128,384]{2,1,0:T(8,128)(2,1)S(1)}, u32[]{:S(2)}, u32[]{:S(2)}) collective-permute-start(bf16[4,128,384]{2,1,0:T(8,128)(2,1)S(1)} %select_select_fusion.15), channel_id=1, source_target_pairs={{0,4},{4,0},{8,12},{12,8},{16,20},{20,16},{24,28},{28,24},{1,5},{5... | collective-permute-start | bytes 1179656 | tf_op jit(solution)/shard_map/ppermute | solution.py:439
  246.5 14.6 %collective-permute-start.27 = (bf16[4,128,384]{2,1,0:T(8,128)(2,1)S(1)}, bf16[4,128,384]{2,1,0:T(8,128)(2,1)S(1)}, u32[]{:S(2)}, u32[]{:S(2)}) collective-permute-start(bf16[4,128,384]{2,1,0:T(8,128)(2,1)S(1)} %get-tuple-element.140), channel_id=1, source_target_pairs={{0,8},{4,12},{8,16},{12,20},{16,24},{20,28},{1,9},{5,13},{9,17},{1... | collective-permute-start | bytes 1179656 | tf_op jit(solution)/shard_map/ppermute | solution.py:432
  262.9 18.0 %collective-permute-start.36 = (bf16[4,128,384]{2,1,0:T(8,128)(2,1)S(1)}, bf16[4,128,384]{2,1,0:T(8,128)(2,1)S(1)}, u32[]{:S(2)}, u32[]{:S(2)}) collective-permute-start(bf16[4,128,384]{2,1,0:T(8,128)(2,1)S(1)} %select_select_fusion.13), channel_id=1, source_target_pairs={{0,4},{4,0},{8,12},{12,8},{16,20},{20,16},{24,28},{28,24},{1,5},{5... | collective-permute-start | bytes 1179656 | tf_op jit(solution)/shard_map/ppermute | solution.py:439
  264.4 14.7 %collective-permute-start.32 = (bf16[4,128,384]{2,1,0:T(8,128)(2,1)S(1)}, bf16[4,128,384]{2,1,0:T(8,128)(2,1)S(1)}, u32[]{:S(2)}, u32[]{:S(2)}) collective-permute-start(bf16[4,128,384]{2,1,0:T(8,128)(2,1)S(1)} %get-tuple-element.148), channel_id=1, source_target_pairs={{0,8},{4,12},{8,16},{12,20},{16,24},{20,28},{1,9},{5,13},{9,17},{1... | collective-permute-start | bytes 1179656 | tf_op jit(solution)/shard_map/ppermute | solution.py:432
  280.9 17.1 %collective-permute-start.31 = (bf16[4,128,384]{2,1,0:T(8,128)(2,1)S(1)}, bf16[4,128,384]{2,1,0:T(8,128)(2,1)S(1)}, u32[]{:S(2)}, u32[]{:S(2)}) collective-permute-start(bf16[4,128,384]{2,1,0:T(8,128)(2,1)S(1)} %select_select_fusion.14), channel_id=1, source_target_pairs={{0,4},{4,0},{8,12},{12,8},{16,20},{20,16},{24,28},{28,24},{1,5},{5... | collective-permute-start | bytes 1179656 | tf_op jit(solution)/shard_map/ppermute | solution.py:439
  281.7 14.6 %collective-permute-start.34 = (bf16[4,128,384]{2,1,0:T(8,128)(2,1)S(1)}, bf16[4,128,384]{2,1,0:T(8,128)(2,1)S(1)}, u32[]{:S(2)}, u32[]{:S(2)}) collective-permute-start(bf16[4,128,384]{2,1,0:T(8,128)(2,1)S(1)} %get-tuple-element.150), channel_id=1, source_target_pairs={{0,8},{4,12},{8,16},{12,20},{16,24},{20,28},{1,9},{5,13},{9,17},{1... | collective-permute-start | bytes 1179656 | tf_op jit(solution)/shard_map/ppermute | solution.py:432
  298.1 17.8 %collective-permute-start.44 = (bf16[4,128,384]{2,1,0:T(8,128)(2,1)S(1)}, bf16[4,128,384]{2,1,0:T(8,128)(2,1)S(1)}, u32[]{:S(2)}, u32[]{:S(2)}) collective-permute-start(bf16[4,128,384]{2,1,0:T(8,128)(2,1)S(1)} %select_select_fusion.11), channel_id=1, source_target_pairs={{0,4},{4,0},{8,12},{12,8},{16,20},{20,16},{24,28},{28,24},{1,5},{5... | collective-permute-start | bytes 1179656 | tf_op jit(solution)/shard_map/ppermute | solution.py:439
  315.9 17.3 %collective-permute-start.39 = (bf16[4,128,384]{2,1,0:T(8,128)(2,1)S(1)}, bf16[4,128,384]{2,1,0:T(8,128)(2,1)S(1)}, u32[]{:S(2)}, u32[]{:S(2)}) collective-permute-start(bf16[4,128,384]{2,1,0:T(8,128)(2,1)S(1)} %select_select_fusion.12), channel_id=1, source_target_pairs={{0,4},{4,0},{8,12},{12,8},{16,20},{20,16},{24,28},{28,24},{1,5},{5... | collective-permute-start | bytes 1179656 | tf_op jit(solution)/shard_map/ppermute | solution.py:439
  316.6 14.8 %collective-permute-start.42 = (bf16[4,128,384]{2,1,0:T(8,128)(2,1)S(1)}, bf16[4,128,384]{2,1,0:T(8,128)(2,1)S(1)}, u32[]{:S(2)}, u32[]{:S(2)}) collective-permute-start(bf16[4,128,384]{2,1,0:T(8,128)(2,1)S(1)} %get-tuple-element.168), channel_id=1, source_target_pairs={{0,8},{4,12},{8,16},{12,20},{16,24},{20,28},{1,9},{5,13},{9,17},{1... | collective-permute-start | bytes 1179656 | tf_op jit(solution)/shard_map/ppermute | solution.py:432
  333.2 16.7 %collective-permute-start.47 = (bf16[4,128,384]{2,1,0:T(8,128)(2,1)S(1)}, bf16[4,128,384]{2,1,0:T(8,128)(2,1)S(1)}, u32[]{:S(2)}, u32[]{:S(2)}) collective-permute-start(bf16[4,128,384]{2,1,0:T(8,128)(2,1)S(1)} %select_select_fusion.9), channel_id=1, source_target_pairs={{0,4},{4,0},{8,12},{12,8},{16,20},{20,16},{24,28},{28,24},{1,5},{5... | collective-permute-start | bytes 1179656 | tf_op jit(solution)/shard_map/ppermute | solution.py:439
  334.6 15.3 %collective-permute-start.48 = (bf16[4,128,384]{2,1,0:T(8,128)(2,1)S(1)}, bf16[4,128,384]{2,1,0:T(8,128)(2,1)S(1)}, u32[]{:S(2)}, u32[]{:S(2)}) collective-permute-start(bf16[4,128,384]{2,1,0:T(8,128)(2,1)S(1)} %get-tuple-element.182), channel_id=1, source_target_pairs={{0,8},{4,12},{8,16},{12,20},{16,24},{20,28},{1,9},{5,13},{9,17},{1... | collective-permute-start | bytes 1179656 | tf_op jit(solution)/shard_map/ppermute | solution.py:432
  351.7 27.9 %collective-permute-start.51 = (bf16[4,128,384]{2,1,0:T(8,128)(2,1)S(1)}, bf16[4,128,384]{2,1,0:T(8,128)(2,1)S(1)}, u32[]{:S(2)}, u32[]{:S(2)}) collective-permute-start(bf16[4,128,384]{2,1,0:T(8,128)(2,1)S(1)} %select_select_fusion.7), channel_id=1, source_target_pairs={{0,4},{4,0},{8,12},{12,8},{16,20},{20,16},{24,28},{28,24},{1,5},{5... | collective-permute-start | bytes 1179656 | tf_op jit(solution)/shard_map/ppermute | solution.py:439
  (96 other events, 571.3 us)

commit v3 on v2

--- a/solution.py
+++ b/solution.py
@@ -19,6 +19,7 @@
 ROWS = 32
 SPLIT = 2
 SKEW = 2
+TURN_VMEM = 50
 MIB = 1024 * 1024
 
 
@@ -201,7 +202,7 @@
         functools.partial(turn_kernel, panels, odd_first, count),
         grid_spec=spec,
         out_shape=[block] * 3,
-        compiler_params=pltpu.CompilerParams(vmem_limit_bytes=40 * MIB),
+        compiler_params=pltpu.CompilerParams(vmem_limit_bytes=TURN_VMEM * MIB),
         cost_estimate=pl.CostEstimate(
             flops=steps * 2 * STACK * BAND * LANES * 2,
             bytes_accessed=steps * STACK * BAND * 2 * 3,
@@ -372,6 +373,7 @@
         mine_too = [own[:1], own[1 : panels - 1], own[panels - 1 :]]
     else:
         other, mine_too = [other_rim], [own]
+    other_rim, mixing, mine = lax.optimization_barrier((other_rim, mixing, mine))
     other_inner_edge, other_outer_edge = both_edges(other_rim, 1)
     even_inner = jnp.where(odd_home, other_inner_edge, own_inner)
     even_outer = jnp.where(odd_home, other_outer_edge, own_outer)

time: 421 us -> 395 us (0.938)
  local copies, waits for them, and re-layouts: 59.8 us -> 36.9 us
  other arithmetic: 20.6 us -> 14 us
  starting transfers between devices: 78 us -> 83.1 us
  waiting for transfers between devices: 42.2 us -> 37.6 us
    unnamed x152 -> x72, local copies, waits for them, and re-layouts: 36.6 us -> 19.7 us
    ppermute x1, waiting for transfers between devices: 11.1 us -> 3.69 us  [on_device(): other_rim = lax.ppermute(rim, 'col', swap)]
    another operation x4, local copies, waits for them, and re-layouts: 9.36 us -> 4.48 us  [on_device(): jnp.stack([mixing_of(jnp.where(odd_home, small_other, small)), mixing_of(...]
    ppermute x15, starting transfers between devices: 26.8 us -> 31.2 us  [inner_edge(): return lax.ppermute(side(block, width, dim, True), 'sec', pairs)]
    dynamic_slice x25 -> x26, local copies, waits for them, and re-layouts: 8.7 us -> 7.59 us  [side(): return lax.dynamic_slice_in_dim(block, start, width, dim)]
  transfers between devices with their start and end apart: 56 -> 56, of which waited for: 5 -> 5; matrix products, arithmetic and copies ran while one was open for 10% -> 8% of each run, Pallas kernels for 44% -> 47%
where the time goes in v3:
time: 395 us; the launch traced here: 388 us
  Pallas kernels  199 us (50%)
  starting transfers between devices  83.1 us (21%)
  waiting for transfers between devices  37.6 us (10%)
  local copies, waits for them, and re-layouts  36.9 us (9%)
  other arithmetic  14 us (4%)
  matrix products  13.8 us (3%)
    pallas_call x14, Pallas kernels, one_turn(): pl.pallas_call(functools.partial(turn_kernel, panels, odd_first, count),...  175 us
    ppermute x15, starting transfers between devices, inner_edge(): return lax.ppermute(side(block, width, dim, True), 'sec', pairs)  31.2 us
    ppermute x12, starting transfers between devices, on_device(): nxt = lax.ppermute(passed, 'col', up)  26.2 us
    ppermute x1, waiting for transfers between devices, on_device(): other_inner = lax.ppermute(inner, 'col', swap)  19.9 us
    unnamed x72, local copies, waits for them, and re-layouts  19.7 us
    pallas_call x4, Pallas kernels, unpacked(): pl.pallas_call(unpack_kernel, grid_spec=pltpu.PrefetchScalarGridSpec(num_...  16 us
    ppermute x1, waiting for transfers between devices, on_device(): lax.ppermute(far_now, 'sec', [(i, i ^ group) for i in range(sec_count)])  12.4 us
    dot_general x2, matrix products, on_device(): lax.dot_general(columns, flat, (((0,), (0,)), ((), ())), preferred_elemen...  10.6 us
  transfers between devices with their start and end apart: 56, of which 5 were waited for; matrix products, arithmetic and copies ran while one was open for 8% of the time, Pallas kernels for 47%

profile of v3, /device:TPU:0, one launch (start us, length us, event | category | flops | bytes accessed | tf_op | source)
XLA Modules:
  0.0 387.6 jit_solution(14529747036432520851)
XLA Ops:
  2.8 2.9 collective-permute-start.3
  9.5 5.3 %order_coupling.1 = bf16[4,768,384]{2,1,0:T(8,128)(2,1)S(1)} custom-call(f32[4,18]{1,0:T(4,128)S(1)} %reshape.49.sign_ref, bf16[512,2304]{1,0:T(8,128)(2,1)S(1)} %bitcast.72, bf16[768,768]{1,0:T(8,128)(2,1)S(1)} %fusion.2.perm_ref), custom_call_target="tpu_custom_call" | custom-call | tf_op jit(solution)/shard_map/order_coupling/pallas_call | solution.py:43
  20.9 2.8 copy-done.5
  23.7 3.4 pack.1.left_ref
  30.8 2.8 collective-permute-start
  43.1 3.7 collective-permute-done.2
  48.9 2.9 collective-permute-start.6
  51.8 19.9 %collective-permute-done.8 = bf16[2,768,384]{2,1,0:T(8,128)(2,1)} collective-permute-done((bf16[2,768,384]{2,1,0:T(8,128)(2,1)}, bf16[2,768,384]{2,1,0:T(8,128)(2,1)}, u32[]{:S(2)}, u32[]{:S(2)}) %collective-permute-start.8) | collective-permute-done | bytes 1179680 | tf_op jit(solution)/shard_map/ppermute | solution.py:371
  81.3 12.4 %two_columns.14 = (bf16[4,128,384]{2,1,0:T(8,128)(2,1)S(1)}, bf16[4,128,384]{2,1,0:T(8,128)(2,1)S(1)}, bf16[4,128,384]{2,1,0:T(8,128)(2,1)S(1)}) custom-call(s32[4]{0:T(128)S(1)} %get-tuple-element.253.flag_ref, bf16[8,2,128,384]{3,2,1,0:T(8,128)(2,1)} %collective-permute-done.left_in_ref, bf16[8,4,128,384]{3,2,1,0:T(8,128)(2,1)} %copy-done.2, ...), custom_call_target="tpu_custom_call" | custom-call | flops 4529848320 | bytes 17694720 | tf_op jit(solution)/shard_map/two_columns/pallas_call | solution.py:201
  94.5 3.5 collective-permute-start.9
  98.7 12.4 %two_columns.15 = (bf16[4,128,384]{2,1,0:T(8,128)(2,1)S(1)}, bf16[4,128,384]{2,1,0:T(8,128)(2,1)S(1)}, bf16[4,128,384]{2,1,0:T(8,128)(2,1)S(1)}) custom-call(s32[4]{0:T(128)S(1)} %get-tuple-element.252.flag_ref, bf16[8,2,128,384]{3,2,1,0:T(8,128)(2,1)} %collective-permute-done.left_in_ref, bf16[8,4,128,384]{3,2,1,0:T(8,128)(2,1)} %copy-done.2, ...), custom_call_target="tpu_custom_call" | custom-call | flops 4529848320 | bytes 17694720 | tf_op jit(solution)/shard_map/two_columns/pallas_call | solution.py:201
  112.7 11.2 %collective-permute-start.13 = (bf16[2,128,384]{2,1,0:T(8,128)(2,1)S(1)}, bf16[2,128,384]{2,1,0:T(8,128)(2,1)S(1)}, u32[]{:S(2)}, u32[]{:S(2)}) collective-permute-start(bf16[2,128,384]{2,1,0:T(8,128)(2,1)S(1)} %constant_dynamic-slice_fusion.22), channel_id=1, source_target_pairs={{0,1},{1,0},{2,3},{3,2},{4,5},{5,4},{6,7},{7,6},{8,9},{9,8},{10,11... | collective-permute-start | bytes 589832 | tf_op jit(solution)/shard_map/ppermute | solution.py:304
  123.9 3.5 collective-permute-start.11
  128.2 12.4 %two_columns.16 = (bf16[4,128,384]{2,1,0:T(8,128)(2,1)S(1)}, bf16[4,128,384]{2,1,0:T(8,128)(2,1)S(1)}, bf16[4,128,384]{2,1,0:T(8,128)(2,1)S(1)}) custom-call(s32[4]{0:T(128)S(1)} %get-tuple-element.251.flag_ref, bf16[8,2,128,384]{3,2,1,0:T(8,128)(2,1)} %collective-permute-done.left_in_ref, bf16[8,4,128,384]{3,2,1,0:T(8,128)(2,1)} %copy-done.2, ...), custom_call_target="tpu_custom_call" | custom-call | flops 4529848320 | bytes 17694720 | tf_op jit(solution)/shard_map/two_columns/pallas_call | solution.py:201
  145.8 12.4 %two_columns.17 = (bf16[4,128,384]{2,1,0:T(8,128)(2,1)S(1)}, bf16[4,128,384]{2,1,0:T(8,128)(2,1)S(1)}, bf16[4,128,384]{2,1,0:T(8,128)(2,1)S(1)}) custom-call(s32[4]{0:T(128)S(1)} %get-tuple-element.250.flag_ref, bf16[8,2,128,384]{3,2,1,0:T(8,128)(2,1)} %collective-permute-done.left_in_ref, bf16[8,4,128,384]{3,2,1,0:T(8,128)(2,1)} %copy-done.2, ...), custom_call_target="tpu_custom_call" | custom-call | flops 4529848320 | bytes 17694720 | tf_op jit(solution)/shard_map/two_columns/pallas_call | solution.py:201
  162.3 12.4 %two_columns.18 = (bf16[4,128,384]{2,1,0:T(8,128)(2,1)S(1)}, bf16[4,128,384]{2,1,0:T(8,128)(2,1)S(1)}, bf16[4,128,384]{2,1,0:T(8,128)(2,1)S(1)}) custom-call(s32[4]{0:T(128)S(1)} %get-tuple-element.249.flag_ref, bf16[8,2,128,384]{3,2,1,0:T(8,128)(2,1)} %collective-permute-done.left_in_ref, bf16[8,4,128,384]{3,2,1,0:T(8,128)(2,1)} %copy-done.2, ...), custom_call_target="tpu_custom_call" | custom-call | flops 4529848320 | bytes 17694720 | tf_op jit(solution)/shard_map/two_columns/pallas_call | solution.py:201
  184.3 12.4 %two_columns.19 = (bf16[4,128,384]{2,1,0:T(8,128)(2,1)S(1)}, bf16[4,128,384]{2,1,0:T(8,128)(2,1)S(1)}, bf16[4,128,384]{2,1,0:T(8,128)(2,1)S(1)}) custom-call(s32[4]{0:T(128)S(1)} %get-tuple-element.248.flag_ref, bf16[8,2,128,384]{3,2,1,0:T(8,128)(2,1)} %collective-permute-done.left_in_ref, bf16[8,4,128,384]{3,2,1,0:T(8,128)(2,1)} %copy-done.2, ...), custom_call_target="tpu_custom_call" | custom-call | flops 4529848320 | bytes 17694720 | tf_op jit(solution)/shard_map/two_columns/pallas_call | solution.py:201
  204.0 12.4 %two_columns.20 = (bf16[4,128,384]{2,1,0:T(8,128)(2,1)S(1)}, bf16[4,128,384]{2,1,0:T(8,128)(2,1)S(1)}, bf16[4,128,384]{2,1,0:T(8,128)(2,1)S(1)}) custom-call(s32[4]{0:T(128)S(1)} %get-tuple-element.254.flag_ref, bf16[8,2,128,384]{3,2,1,0:T(8,128)(2,1)} %collective-permute-done.left_in_ref, bf16[8,4,128,384]{3,2,1,0:T(8,128)(2,1)} %copy-done.2, ...), custom_call_target="tpu_custom_call" | custom-call | flops 4529848320 | bytes 17694720 | tf_op jit(solution)/shard_map/two_columns/pallas_call | solution.py:201
  220.6 12.4 %two_columns.21 = (bf16[4,128,384]{2,1,0:T(8,128)(2,1)S(1)}, bf16[4,128,384]{2,1,0:T(8,128)(2,1)S(1)}, bf16[4,128,384]{2,1,0:T(8,128)(2,1)S(1)}) custom-call(s32[4]{0:T(128)S(1)} %get-tuple-element.246.flag_ref, bf16[8,2,128,384]{3,2,1,0:T(8,128)(2,1)} %collective-permute-done.left_in_ref, bf16[8,4,128,384]{3,2,1,0:T(8,128)(2,1)} %copy-done.2, ...), custom_call_target="tpu_custom_call" | custom-call | flops 4529848320 | bytes 17694720 | tf_op jit(solution)/shard_map/two_columns/pallas_call | solution.py:201
  239.2 12.4 %two_columns.22 = (bf16[4,128,384]{2,1,0:T(8,128)(2,1)S(1)}, bf16[4,128,384]{2,1,0:T(8,128)(2,1)S(1)}, bf16[4,128,384]{2,1,0:T(8,128)(2,1)S(1)}) custom-call(s32[4]{0:T(128)S(1)} %get-tuple-element.143.flag_ref, bf16[8,2,128,384]{3,2,1,0:T(8,128)(2,1)} %collective-permute-done.left_in_ref, bf16[8,4,128,384]{3,2,1,0:T(8,128)(2,1)} %copy-done.2, ...), custom_call_target="tpu_custom_call" | custom-call | flops 4529848320 | bytes 17694720 | tf_op jit(solution)/shard_map/two_columns/pallas_call | solution.py:201
  256.0 12.4 %two_columns.23 = (bf16[4,128,384]{2,1,0:T(8,128)(2,1)S(1)}, bf16[4,128,384]{2,1,0:T(8,128)(2,1)S(1)}, bf16[4,128,384]{2,1,0:T(8,128)(2,1)S(1)}) custom-call(s32[4]{0:T(128)S(1)} %get-tuple-element.161.flag_ref, bf16[8,2,128,384]{3,2,1,0:T(8,128)(2,1)} %collective-permute-done.left_in_ref, bf16[8,4,128,384]{3,2,1,0:T(8,128)(2,1)} %copy-done.2, ...), custom_call_target="tpu_custom_call" | custom-call | flops 4529848320 | bytes 17694720 | tf_op jit(solution)/shard_map/two_columns/pallas_call | solution.py:201
  274.6 12.4 %two_columns.24 = (bf16[4,128,384]{2,1,0:T(8,128)(2,1)S(1)}, bf16[4,128,384]{2,1,0:T(8,128)(2,1)S(1)}, bf16[4,128,384]{2,1,0:T(8,128)(2,1)S(1)}) custom-call(s32[4]{0:T(128)S(1)} %add_add_fusion.flag_ref, bf16[8,2,128,384]{3,2,1,0:T(8,128)(2,1)} %collective-permute-done.left_in_ref, bf16[8,4,128,384]{3,2,1,0:T(8,128)(2,1)} %copy-done.2, ...), custom_call_target="tpu_custom_call" | custom-call | flops 4529848320 | bytes 17694720 | tf_op jit(solution)/shard_map/two_columns/pallas_call | solution.py:201
  291.3 12.4 %two_columns.25 = (bf16[4,128,384]{2,1,0:T(8,128)(2,1)S(1)}, bf16[4,128,384]{2,1,0:T(8,128)(2,1)S(1)}, bf16[4,128,384]{2,1,0:T(8,128)(2,1)S(1)}) custom-call(s32[4]{0:T(128)S(1)} %get-tuple-element.176.flag_ref, bf16[8,2,128,384]{3,2,1,0:T(8,128)(2,1)} %collective-permute-done.left_in_ref, bf16[8,4,128,384]{3,2,1,0:T(8,128)(2,1)} %copy-done.2, ...), custom_call_target="tpu_custom_call" | custom-call | flops 4529848320 | bytes 17694720 | tf_op jit(solution)/shard_map/two_columns/pallas_call | solution.py:201
  310.1 13.1 %two_columns.26 = (bf16[4,128,384]{2,1,0:T(8,128)(2,1)S(1)}, bf16[4,128,384]{2,1,0:T(8,128)(2,1)S(1)}, bf16[4,128,384]{2,1,0:T(8,128)(2,1)}) custom-call(s32[4]{0:T(128)S(1)} %get-tuple-element.171.flag_ref, bf16[8,2,128,384]{3,2,1,0:T(8,128)(2,1)} %collective-permute-done.left_in_ref, bf16[8,4,128,384]{3,2,1,0:T(8,128)(2,1)} %copy-done.2, ...), custom_call_target="tpu_custom_call" | custom-call | flops 4529848320 | bytes 17694720 | tf_op jit(solution)/shard_map/two_columns/pallas_call | solution.py:201
  325.7 13.1 %two_columns.27 = (bf16[4,128,384]{2,1,0:T(8,128)(2,1)S(1)}, bf16[4,128,384]{2,1,0:T(8,128)(2,1)S(1)}, bf16[4,128,384]{2,1,0:T(8,128)(2,1)}) custom-call(s32[4]{0:T(128)S(1)} %get-tuple-element.187.flag_ref, bf16[8,2,128,384]{3,2,1,0:T(8,128)(2,1)} %collective-permute-done.left_in_ref, bf16[8,4,128,384]{3,2,1,0:T(8,128)(2,1)} %copy-done.2, ...), custom_call_target="tpu_custom_call" | custom-call | flops 4529848320 | bytes 17694720 | tf_op jit(solution)/shard_map/two_columns/pallas_call | solution.py:201
  340.8 3.9 %unpack.4.rest_0_ = bf16[6,512,1024]{2,1,0:T(8,128)(2,1)} custom-call(s32[2]{0:T(128)S(1)} %get-tuple-element.209.at_ref, bf16[4,128,384]{2,1,0:T(8,128)(2,1)S(1)} %get-tuple-element.228.ka_ref, bf16[4,128,384]{2,1,0:T(8,128)(2,1)S(1)} %get-tuple-element.224.kb_ref, bf16[4,128,384]{2,1,0:T(8,128)(2,1)S(1)} %collective-permute-done.24.ga_ref, ...), custom_call_target="tpu_custom_call" | custom-call | tf_op jit(solution)/shard_map/unpack/pallas_call | solution.py:260
  344.7 3.9 %unpack.5.rest_0_ = bf16[6,512,1024]{2,1,0:T(8,128)(2,1)} custom-call(s32[2]{0:T(128)S(1)} %get-tuple-element.208.at_ref, bf16[4,128,384]{2,1,0:T(8,128)(2,1)S(1)} %get-tuple-element.229.ka_ref, bf16[4,128,384]{2,1,0:T(8,128)(2,1)S(1)} %get-tuple-element.225.kb_ref, ...), custom_call_target="tpu_custom_call", output_to_operand_aliasing={{}: (5, {})} | custom-call | tf_op jit(solution)/shard_map/unpack/pallas_call | solution.py:260
  348.7 3.9 %unpack.6.rest_0_ = bf16[6,512,1024]{2,1,0:T(8,128)(2,1)} custom-call(s32[2]{0:T(128)S(1)} %get-tuple-element.241.at_ref, bf16[4,128,384]{2,1,0:T(8,128)(2,1)S(1)} %get-tuple-element.230.ka_ref, bf16[4,128,384]{2,1,0:T(8,128)(2,1)S(1)} %get-tuple-element.226.kb_ref, ...), custom_call_target="tpu_custom_call", output_to_operand_aliasing={{}: (5, {})} | custom-call | tf_op jit(solution)/shard_map/unpack/pallas_call | solution.py:260
  352.6 4.2 %unpack.7 = bf16[6,512,1024]{2,1,0:T(8,128)(2,1)} custom-call(s32[2]{0:T(128)S(1)} %get-tuple-element.242.at_ref, bf16[4,128,384]{2,1,0:T(8,128)(2,1)S(1)} %get-tuple-element.231.ka_ref, bf16[4,128,384]{2,1,0:T(8,128)(2,1)S(1)} %get-tuple-element.227.kb_ref, bf16[4,128,384]{2,1,0:T(8,128)(2,1)S(1)} %collective-permute-done.51.ga_ref, ...), custom_call_target="tpu_custom_call", output_to_operand_aliasing={{}: (5, {})} | custom-call | tf_op jit(solution)/shard_map/unpack/pallas_call | solution.py:260
  356.8 7.2 %fusion.3 = bf16[512,1024]{1,0:T(8,128)(2,1)S(1)} fusion(bf16[3072,1024]{1,0:T(8,128)(2,1)} %bitcast.73, s32[]{:T(128)S(6)} %select_n.561), kind=kOutput, calls=%fused_computation.4 | convolution fusion | flops 3221749760 | bytes 10485764 | tf_op jit(solution)/shard_map/dot_general | solution.py:460
  367.9 3.4 convolution_convert_fusion
  373.5 12.4 %collective-permute-done.55 = bf16[1,256,1024]{2,1,0:T(8,128)(2,1)S(1)} collective-permute-done((bf16[1,256,1024]{2,1,0:T(8,128)(2,1)S(1)}, bf16[1,256,1024]{2,1,0:T(8,128)(2,1)S(1)}, u32[]{:S(2)}, u32[]{:S(2)}) %collective-permute-start.55) | collective-permute-done | bytes 524320 | tf_op jit(solution)/shard_map/ppermute | solution.py:459
  (261 shorter events, 109.3 us)
Async XLA Ops:
  2.8 28.0 %collective-permute-start.3 = (f32[6,1240]{1,0:T(8,128)S(1)}, f32[6,1240]{1,0:T(8,128)S(1)}, u32[]{:S(2)}, u32[]{:S(2)}) collective-permute-start(f32[6,1240]{1,0:T(8,128)S(1)} %pad_maximum_fusion.2), channel_id=1, source_target_pairs={{0,4},{4,0},{8,12},{12,8},{16,20},{20,16},{24,28},{28,24},{1,5},{5... | collective-permute-start | bytes 89288 | tf_op jit(solution)/shard_map/ppermute | solution.py:348
  16.6 32.3 %collective-permute-start.7 = (bf16[1,768,384]{2,1,0:T(8,128)(2,1)}, bf16[1,768,384]{2,1,0:T(8,128)(2,1)}, u32[]{:S(2)}, u32[]{:S(2)}) collective-permute-start(bf16[1,768,384]{2,1,0:T(8,128)(2,1)} %get-tuple-element.232), channel_id=1, source_target_pairs={{0,1},{1,0},{2,3},{3,2},{4,5},{5,4},{6,7},{7,6},{8,9},{9,8},{10,11... | collective-permute-start | bytes 1769480 | tf_op jit(solution)/shard_map/ppermute | solution.py:304
  17.7 29.1 %collective-permute-start.2 = (bf16[2,768,384]{2,1,0:T(8,128)(2,1)}, bf16[2,768,384]{2,1,0:T(8,128)(2,1)}, u32[]{:S(2)}, u32[]{:S(2)}) collective-permute-start(bf16[2,768,384]{2,1,0:T(8,128)(2,1)} %pad_maximum_fusion), channel_id=1, source_target_pairs={{0,4},{4,0},{8,12},{12,8},{16,20},{20,16},{24,28},{28,24},{1,5},{5... | collective-permute-start | bytes 3538952 | tf_op jit(solution)/shard_map/ppermute | solution.py:344
  18.9 52.8 %collective-permute-start.8 = (bf16[2,768,384]{2,1,0:T(8,128)(2,1)}, bf16[2,768,384]{2,1,0:T(8,128)(2,1)}, u32[]{:S(2)}, u32[]{:S(2)}) collective-permute-start(bf16[2,768,384]{2,1,0:T(8,128)(2,1)} %slice.48), channel_id=1, source_target_pairs={{0,4},{4,0},{8,12},{12,8},{16,20},{20,16},{24,28},{28,24},{1,5},{5... | collective-permute-start | bytes 3538952 | tf_op jit(solution)/shard_map/ppermute | solution.py:371
  29.8 47.1 %collective-permute-start.1 = (bf16[8,2,128,384]{3,2,1,0:T(8,128)(2,1)}, bf16[8,2,128,384]{3,2,1,0:T(8,128)(2,1)S(1)}, u32[]{:S(2)}, u32[]{:S(2)}) collective-permute-start(bf16[8,2,128,384]{3,2,1,0:T(8,128)(2,1)} %get-tuple-element.218), channel_id=1, source_target_pairs={{1,2},{2,1},{5,6},{6,5},{9,10},{10,9},{13,14},{14,13},{17,18},{18,... | collective-permute-start | bytes 4718600 | tf_op jit(solution)/shard_map/ppermute | solution.py:316
  30.8 46.1 %collective-permute-start = (bf16[8,2,128,384]{3,2,1,0:T(8,128)(2,1)}, bf16[8,2,128,384]{3,2,1,0:T(8,128)(2,1)}, u32[]{:S(2)}, u32[]{:S(2)}) collective-permute-start(bf16[8,2,128,384]{3,2,1,0:T(8,128)(2,1)} %get-tuple-element.219), channel_id=1, source_target_pairs={{0,1},{1,0},{2,3},{3,2},{4,5},{5,4},{6,7},{7,6},{8,9},{9,8},{10,11... | collective-permute-start | bytes 4718600 | tf_op jit(solution)/shard_map/ppermute | solution.py:304
  46.8 28.8 %collective-permute-start.5 = (bf16[1,768,384]{2,1,0:T(8,128)(2,1)}, bf16[1,768,384]{2,1,0:T(8,128)(2,1)S(1)}, u32[]{:S(2)}, u32[]{:S(2)}) collective-permute-start(bf16[1,768,384]{2,1,0:T(8,128)(2,1)} %get-tuple-element.233), channel_id=1, source_target_pairs={{1,2},{2,1},{5,6},{6,5},{9,10},{10,9},{13,14},{14,13},{17,18},{18,... | collective-permute-start | bytes 1769480 | tf_op jit(solution)/shard_map/ppermute | solution.py:316
  48.9 26.7 %collective-permute-start.6 = (bf16[1,768,384]{2,1,0:T(8,128)(2,1)S(1)}, bf16[1,768,384]{2,1,0:T(8,128)(2,1)S(1)}, u32[]{:S(2)}, u32[]{:S(2)}) collective-permute-start(bf16[1,768,384]{2,1,0:T(8,128)(2,1)S(1)} %get-tuple-element.234), channel_id=1, source_target_pairs={{0,1},{1,0},{2,3},{3,2},{4,5},{5,4},{6,7},{7,6},{8,9},{9,8},{10,11... | collective-permute-start | bytes 1769480 | tf_op jit(solution)/shard_map/ppermute | solution.py:304
  94.5 18.2 %collective-permute-start.9 = (bf16[4,128,384]{2,1,0:T(8,128)(2,1)S(1)}, bf16[4,128,384]{2,1,0:T(8,128)(2,1)S(1)}, u32[]{:S(2)}, u32[]{:S(2)}) collective-permute-start(bf16[4,128,384]{2,1,0:T(8,128)(2,1)S(1)} %get-tuple-element.119), channel_id=1, source_target_pairs={{0,8},{4,12},{8,16},{12,20},{16,24},{20,28},{1,9},{5,13},{9,17},{1... | collective-permute-start | bytes 1179656 | tf_op jit(solution)/shard_map/ppermute | solution.py:434
  98.0 14.7 %collective-permute-start.10 = (bf16[2,128,384]{2,1,0:T(8,128)(2,1)S(1)}, bf16[2,128,384]{2,1,0:T(8,128)(2,1)S(1)}, u32[]{:S(2)}, u32[]{:S(2)}) collective-permute-start(bf16[2,128,384]{2,1,0:T(8,128)(2,1)S(1)} %constant_dynamic-slice_fusion.24), channel_id=1, source_target_pairs={{1,10},{2,9},{5,14},{6,13},{9,18},{10,17},{13,22},{14,21},{17,26},... | collective-permute-start | bytes 589832 | tf_op jit(solution)/shard_map/ppermute | solution.py:437
  112.7 15.5 %collective-permute-start.13 = (bf16[2,128,384]{2,1,0:T(8,128)(2,1)S(1)}, bf16[2,128,384]{2,1,0:T(8,128)(2,1)S(1)}, u32[]{:S(2)}, u32[]{:S(2)}) collective-permute-start(bf16[2,128,384]{2,1,0:T(8,128)(2,1)S(1)} %constant_dynamic-slice_fusion.22), channel_id=1, source_target_pairs={{0,1},{1,0},{2,3},{3,2},{4,5},{5,4},{6,7},{7,6},{8,9},{9,8},{10,11... | collective-permute-start | bytes 589832 | tf_op jit(solution)/shard_map/ppermute | solution.py:304
  123.9 17.4 %collective-permute-start.11 = (bf16[4,128,384]{2,1,0:T(8,128)(2,1)S(1)}, bf16[4,128,384]{2,1,0:T(8,128)(2,1)S(1)}, u32[]{:S(2)}, u32[]{:S(2)}) collective-permute-start(bf16[4,128,384]{2,1,0:T(8,128)(2,1)S(1)} %get-tuple-element.121), channel_id=1, source_target_pairs={{0,8},{4,12},{8,16},{12,20},{16,24},{20,28},{1,9},{5,13},{9,17},{1... | collective-permute-start | bytes 1179656 | tf_op jit(solution)/shard_map/ppermute | solution.py:434
  142.7 15.5 %collective-permute-start.14 = (bf16[4,128,384]{2,1,0:T(8,128)(2,1)S(1)}, bf16[4,128,384]{2,1,0:T(8,128)(2,1)S(1)}, u32[]{:S(2)}, u32[]{:S(2)}) collective-permute-start(bf16[4,128,384]{2,1,0:T(8,128)(2,1)S(1)} %get-tuple-element.125), channel_id=1, source_target_pairs={{0,8},{4,12},{8,16},{12,20},{16,24},{20,28},{1,9},{5,13},{9,17},{1... | collective-permute-start | bytes 1179656 | tf_op jit(solution)/shard_map/ppermute | solution.py:434
  159.6 15.8 %collective-permute-start.17 = (bf16[4,128,384]{2,1,0:T(8,128)(2,1)S(1)}, bf16[4,128,384]{2,1,0:T(8,128)(2,1)S(1)}, u32[]{:S(2)}, u32[]{:S(2)}) collective-permute-start(bf16[4,128,384]{2,1,0:T(8,128)(2,1)S(1)} %get-tuple-element.129), channel_id=1, source_target_pairs={{0,8},{4,12},{8,16},{12,20},{16,24},{20,28},{1,9},{5,13},{9,17},{1... | collective-permute-start | bytes 1179656 | tf_op jit(solution)/shard_map/ppermute | solution.py:434
  178.1 19.3 %collective-permute-start.20 = (bf16[4,128,384]{2,1,0:T(8,128)(2,1)}, bf16[4,128,384]{2,1,0:T(8,128)(2,1)S(1)}, u32[]{:S(2)}, u32[]{:S(2)}) collective-permute-start(bf16[4,128,384]{2,1,0:T(8,128)(2,1)} %copy-done.28), channel_id=1, source_target_pairs={{0,8},{4,12},{8,16},{12,20},{16,24},{20,28},{1,9},{5,13},{9,17},{1... | collective-permute-start | bytes 1179656 | tf_op jit(solution)/shard_map/ppermute | solution.py:434
  181.1 16.4 %collective-permute-start.21 = (bf16[2,128,384]{2,1,0:T(8,128)(2,1)S(1)}, bf16[2,128,384]{2,1,0:T(8,128)(2,1)S(1)}, u32[]{:S(2)}, u32[]{:S(2)}) collective-permute-start(bf16[2,128,384]{2,1,0:T(8,128)(2,1)S(1)} %constant_dynamic-slice_fusion.17), channel_id=1, source_target_pairs={{1,10},{2,9},{5,14},{6,13},{9,18},{10,17},{13,22},{14,21},{17,26},... | collective-permute-start | bytes 589832 | tf_op jit(solution)/shard_map/ppermute | solution.py:437
  200.2 16.2 %collective-permute-start.25 = (bf16[4,128,384]{2,1,0:T(8,128)(2,1)}, bf16[4,128,384]{2,1,0:T(8,128)(2,1)S(1)}, u32[]{:S(2)}, u32[]{:S(2)}) collective-permute-start(bf16[4,128,384]{2,1,0:T(8,128)(2,1)} %copy-done.27), channel_id=1, source_target_pairs={{0,8},{4,12},{8,16},{12,20},{16,24},{20,28},{1,9},{5,13},{9,17},{1... | collective-permute-start | bytes 1179656 | tf_op jit(solution)/shard_map/ppermute | solution.py:434
  217.8 16.6 %collective-permute-start.24 = (bf16[4,128,384]{2,1,0:T(8,128)(2,1)S(1)}, bf16[4,128,384]{2,1,0:T(8,128)(2,1)S(1)}, u32[]{:S(2)}, u32[]{:S(2)}) collective-permute-start(bf16[4,128,384]{2,1,0:T(8,128)(2,1)S(1)} %select_select_fusion.15), channel_id=1, source_target_pairs={{0,4},{4,0},{8,12},{12,8},{16,20},{20,16},{24,28},{28,24},{1,5},{5... | collective-permute-start | bytes 1179656 | tf_op jit(solution)/shard_map/ppermute | solution.py:441
  217.9 15.1 %collective-permute-start.27 = (bf16[4,128,384]{2,1,0:T(8,128)(2,1)S(1)}, bf16[4,128,384]{2,1,0:T(8,128)(2,1)S(1)}, u32[]{:S(2)}, u32[]{:S(2)}) collective-permute-start(bf16[4,128,384]{2,1,0:T(8,128)(2,1)S(1)} %get-tuple-element.146), channel_id=1, source_target_pairs={{0,8},{4,12},{8,16},{12,20},{16,24},{20,28},{1,9},{5,13},{9,17},{1... | collective-permute-start | bytes 1179656 | tf_op jit(solution)/shard_map/ppermute | solution.py:434
  234.4 18.6 %collective-permute-start.36 = (bf16[4,128,384]{2,1,0:T(8,128)(2,1)S(1)}, bf16[4,128,384]{2,1,0:T(8,128)(2,1)S(1)}, u32[]{:S(2)}, u32[]{:S(2)}) collective-permute-start(bf16[4,128,384]{2,1,0:T(8,128)(2,1)S(1)} %select_select_fusion.13), channel_id=1, source_target_pairs={{0,4},{4,0},{8,12},{12,8},{16,20},{20,16},{24,28},{28,24},{1,5},{5... | collective-permute-start | bytes 1179656 | tf_op jit(solution)/shard_map/ppermute | solution.py:441
  236.5 15.1 %collective-permute-start.32 = (bf16[4,128,384]{2,1,0:T(8,128)(2,1)S(1)}, bf16[4,128,384]{2,1,0:T(8,128)(2,1)S(1)}, u32[]{:S(2)}, u32[]{:S(2)}) collective-permute-start(bf16[4,128,384]{2,1,0:T(8,128)(2,1)S(1)} %get-tuple-element.154), channel_id=1, source_target_pairs={{0,8},{4,12},{8,16},{12,20},{16,24},{20,28},{1,9},{5,13},{9,17},{1... | collective-permute-start | bytes 1179656 | tf_op jit(solution)/shard_map/ppermute | solution.py:434
  253.0 16.8 %collective-permute-start.31 = (bf16[4,128,384]{2,1,0:T(8,128)(2,1)S(1)}, bf16[4,128,384]{2,1,0:T(8,128)(2,1)S(1)}, u32[]{:S(2)}, u32[]{:S(2)}) collective-permute-start(bf16[4,128,384]{2,1,0:T(8,128)(2,1)S(1)} %select_select_fusion.14), channel_id=1, source_target_pairs={{0,4},{4,0},{8,12},{12,8},{16,20},{20,16},{24,28},{28,24},{1,5},{5... | collective-permute-start | bytes 1179656 | tf_op jit(solution)/shard_map/ppermute | solution.py:441
  253.2 15.3 %collective-permute-start.34 = (bf16[4,128,384]{2,1,0:T(8,128)(2,1)S(1)}, bf16[4,128,384]{2,1,0:T(8,128)(2,1)S(1)}, u32[]{:S(2)}, u32[]{:S(2)}) collective-permute-start(bf16[4,128,384]{2,1,0:T(8,128)(2,1)S(1)} %get-tuple-element.156), channel_id=1, source_target_pairs={{0,8},{4,12},{8,16},{12,20},{16,24},{20,28},{1,9},{5,13},{9,17},{1... | collective-permute-start | bytes 1179656 | tf_op jit(solution)/shard_map/ppermute | solution.py:434
  269.9 18.6 %collective-permute-start.44 = (bf16[4,128,384]{2,1,0:T(8,128)(2,1)S(1)}, bf16[4,128,384]{2,1,0:T(8,128)(2,1)S(1)}, u32[]{:S(2)}, u32[]{:S(2)}) collective-permute-start(bf16[4,128,384]{2,1,0:T(8,128)(2,1)S(1)} %select_select_fusion.11), channel_id=1, source_target_pairs={{0,4},{4,0},{8,12},{12,8},{16,20},{20,16},{24,28},{28,24},{1,5},{5... | collective-permute-start | bytes 1179656 | tf_op jit(solution)/shard_map/ppermute | solution.py:441
  272.0 15.1 %collective-permute-start.40 = (bf16[4,128,384]{2,1,0:T(8,128)(2,1)S(1)}, bf16[4,128,384]{2,1,0:T(8,128)(2,1)S(1)}, u32[]{:S(2)}, u32[]{:S(2)}) collective-permute-start(bf16[4,128,384]{2,1,0:T(8,128)(2,1)S(1)} %get-tuple-element.172), channel_id=1, source_target_pairs={{0,8},{4,12},{8,16},{12,20},{16,24},{20,28},{1,9},{5,13},{9,17},{1... | collective-permute-start | bytes 1179656 | tf_op jit(solution)/shard_map/ppermute | solution.py:434
  288.5 16.6 %collective-permute-start.39 = (bf16[4,128,384]{2,1,0:T(8,128)(2,1)S(1)}, bf16[4,128,384]{2,1,0:T(8,128)(2,1)S(1)}, u32[]{:S(2)}, u32[]{:S(2)}) collective-permute-start(bf16[4,128,384]{2,1,0:T(8,128)(2,1)S(1)} %select_select_fusion.12), channel_id=1, source_target_pairs={{0,4},{4,0},{8,12},{12,8},{16,20},{20,16},{24,28},{28,24},{1,5},{5... | collective-permute-start | bytes 1179656 | tf_op jit(solution)/shard_map/ppermute | solution.py:441
  288.6 15.1 %collective-permute-start.42 = (bf16[4,128,384]{2,1,0:T(8,128)(2,1)S(1)}, bf16[4,128,384]{2,1,0:T(8,128)(2,1)S(1)}, u32[]{:S(2)}, u32[]{:S(2)}) collective-permute-start(bf16[4,128,384]{2,1,0:T(8,128)(2,1)S(1)} %get-tuple-element.174), channel_id=1, source_target_pairs={{0,8},{4,12},{8,16},{12,20},{16,24},{20,28},{1,9},{5,13},{9,17},{1... | collective-permute-start | bytes 1179656 | tf_op jit(solution)/shard_map/ppermute | solution.py:434
  305.1 18.1 %collective-permute-start.47 = (bf16[4,128,384]{2,1,0:T(8,128)(2,1)S(1)}, bf16[4,128,384]{2,1,0:T(8,128)(2,1)S(1)}, u32[]{:S(2)}, u32[]{:S(2)}) collective-permute-start(bf16[4,128,384]{2,1,0:T(8,128)(2,1)S(1)} %select_select_fusion.9), channel_id=1, source_target_pairs={{0,4},{4,0},{8,12},{12,8},{16,20},{20,16},{24,28},{28,24},{1,5},{5... | collective-permute-start | bytes 1179656 | tf_op jit(solution)/shard_map/ppermute | solution.py:441
  307.2 16.1 %collective-permute-start.48 = (bf16[4,128,384]{2,1,0:T(8,128)(2,1)S(1)}, bf16[4,128,384]{2,1,0:T(8,128)(2,1)S(1)}, u32[]{:S(2)}, u32[]{:S(2)}) collective-permute-start(bf16[4,128,384]{2,1,0:T(8,128)(2,1)S(1)} %get-tuple-element.188), channel_id=1, source_target_pairs={{0,8},{4,12},{8,16},{12,20},{16,24},{20,28},{1,9},{5,13},{9,17},{1... | collective-permute-start | bytes 1179656 | tf_op jit(solution)/shard_map/ppermute | solution.py:434
  309.2 14.1 %collective-permute-start.49 = (bf16[2,128,384]{2,1,0:T(8,128)(2,1)S(1)}, bf16[2,128,384]{2,1,0:T(8,128)(2,1)S(1)}, u32[]{:S(2)}, u32[]{:S(2)}) collective-permute-start(bf16[2,128,384]{2,1,0:T(8,128)(2,1)S(1)} %constant_dynamic-slice_fusion.2), channel_id=1, source_target_pairs={{1,10},{2,9},{5,14},{6,13},{9,18},{10,17},{13,22},{14,21},{17,26},... | collective-permute-start | bytes 589832 | tf_op jit(solution)/shard_map/ppermute | solution.py:437
  324.8 27.8 %collective-permute-start.51 = (bf16[4,128,384]{2,1,0:T(8,128)(2,1)S(1)}, bf16[4,128,384]{2,1,0:T(8,128)(2,1)S(1)}, u32[]{:S(2)}, u32[]{:S(2)}) collective-permute-start(bf16[4,128,384]{2,1,0:T(8,128)(2,1)S(1)} %select_select_fusion.7), channel_id=1, source_target_pairs={{0,4},{4,0},{8,12},{12,8},{16,20},{20,16},{24,28},{28,24},{1,5},{5... | collective-permute-start | bytes 1179656 | tf_op jit(solution)/shard_map/ppermute | solution.py:441
  371.9 13.9 %collective-permute-start.55 = (bf16[1,256,1024]{2,1,0:T(8,128)(2,1)S(1)}, bf16[1,256,1024]{2,1,0:T(8,128)(2,1)S(1)}, u32[]{:S(2)}, u32[]{:S(2)}) collective-permute-start(bf16[1,256,1024]{2,1,0:T(8,128)(2,1)S(1)} %fusion.8), channel_id=1, source_target_pairs={{0,2},{1,3},{2,0},{3,1},{4,6},{5,7},{6,4},{7,5},{8,10},{9,11},{10,... | collective-permute-start | bytes 1572872 | tf_op jit(solution)/shard_map/ppermute | solution.py:459
  (56 other events, 393.7 us)
